TPU v7x, 32 devices: a whole 2x2x4 slice. The times are simulated.
32 devices in a mesh: section: 2 (over x), ctx: 4 (over y, core), exp: 4 (over z).
Axes of the slice: x: 2, y: 2, z: 4, core: 2. Of those that a mesh axis runs over, the one named last changes fastest.
Arguments:
- queries: bfloat16 [4096, 1024], P('ctx', ('section', 'exp')), may hold values from -6 to 6
- key_rows: bfloat16 [4096, 1024], P('ctx', ('section', 'exp')), may hold values from -0.5 to 0.5
- value_rows: bfloat16 [4096, 1024], P('ctx', ('section', 'exp')), may hold values from -6 to 6
- gate_input: bfloat16 [4096, 1024], P('ctx', ('section', 'exp')), may hold values from -6 to 6
- norm_gain: float32 [1024], P(('section', 'exp')), may hold values from 0.25 to 1.75
- log_decay: float32 [8, 4096], P(('section', 'exp'), 'ctx'), may hold values from -1 to 0, as said below
- grad_output: bfloat16 [4096, 1024], P('ctx', ('section', 'exp')), may hold values from -6 to 6
Outputs:
- layer_out: bfloat16 [4096, 1024], P('ctx', ('section', 'exp'))
- grad_queries: bfloat16 [4096, 1024], P('ctx', ('section', 'exp'))
- grad_keys: bfloat16 [4096, 1024], P('ctx', ('section', 'exp'))
- grad_values: bfloat16 [4096, 1024], P('ctx', ('section', 'exp'))
- grad_gate: bfloat16 [4096, 1024], P('ctx', ('section', 'exp'))
Inputs may be any that keep to these rules, and one draw needn't show every extreme that they name: `log_decay`: each entry is the logarithm of one head's decay factor at one position.
All inputs are finite; a program needn't handle non-finite values.
Results may differ from a plain program's by a relative error of at most 0.0051.
Values sent between devices are 32-bit elements; how exact they have to be, the bound alone decides.
A program may use at most 64 MiB of HBM per device.

v0:
```python
from functools import partial

import jax
import jax.numpy as jnp
from jax import lax
from jax.sharding import PartitionSpec as P

HEAD_DIM = 128


precise = lax.Precision.HIGHEST
epsilon = 1e-06


def entering_2(part, axis, combine, identity, reverse):
    count = lax.axis_size(axis)
    place = lax.axis_index(axis)
    ahead = count - 1 - place if reverse else place
    gathered = jax.tree.map(lambda a: lax.all_gather(a, axis), part)
    state = jax.tree.map(lambda a, e: jnp.zeros_like(a) + jnp.asarray(e, a.dtype), part, identity)

    def one(turn, state):
        source = count - 1 - turn if reverse else turn
        return combine(
            state, jax.tree.map(lambda a: lax.dynamic_index_in_dim(a, source, 0, False), gathered)
        )

    return lax.fori_loop(0, ahead, one, state)


def decay_weights(log_rates):
    cumulated = jnp.cumsum(log_rates)
    length = log_rates.shape[0]
    row_index = lax.broadcasted_iota(jnp.int32, (length, length), 0)
    col_index = lax.broadcasted_iota(jnp.int32, (length, length), 1)
    lower = jnp.exp(jnp.minimum(cumulated[:, None] - cumulated[None, :], 0.0))
    return (cumulated, jnp.where(row_index >= col_index, lower, 0.0))


def block_forward(entering, pieces):
    queries, key_rows, value_rows, log_rates = pieces
    cumulated, weights_table = decay_weights(log_rates)
    scores = jnp.dot(queries, key_rows.T, preferred_element_type=jnp.float32)
    weights = (scores * weights_table).astype(jnp.bfloat16)
    carried = jnp.dot(queries.astype(jnp.float32), entering, precision=precise)
    output = (
        jnp.dot(weights, value_rows, preferred_element_type=jnp.float32)
        + jnp.exp(cumulated)[:, None] * carried
    )
    tail_decay = jnp.exp(cumulated[-1] - cumulated)[:, None]
    update = jnp.dot(
        (key_rows.astype(jnp.float32) * tail_decay).T,
        value_rows.astype(jnp.float32),
        precision=precise,
    )
    leaving = jnp.exp(cumulated[-1]) * entering + update
    return (leaving, (output, entering))


def split_blocks(tensor, block_len):
    return tensor.reshape((tensor.shape[0] // block_len, block_len) + tensor.shape[1:])


def forward_run(queries, key_rows, value_rows, log_rates, start, block_len):
    pieces = tuple((split_blocks(t, block_len) for t in (queries, key_rows, value_rows, log_rates)))
    closing, (outputs, entries) = lax.scan(block_forward, start, pieces)
    return (outputs.reshape(queries.shape), entries, closing)


def block_backward(leaving, pieces):
    queries, key_rows, value_rows, grad_attn, log_rates, entering = pieces
    cumulated, weights_table = decay_weights(log_rates)
    qk_weights = (
        jnp.dot(queries, key_rows.T, preferred_element_type=jnp.float32) * weights_table
    ).astype(jnp.bfloat16)
    dv_weights = (
        jnp.dot(grad_attn, value_rows.T, preferred_element_type=jnp.float32) * weights_table
    ).astype(jnp.bfloat16)
    front_decay = jnp.exp(cumulated)[:, None]
    tail_decay = jnp.exp(cumulated[-1] - cumulated)[:, None]
    grad_float = grad_attn.astype(jnp.float32)
    grad_q = jnp.dot(
        dv_weights, key_rows, preferred_element_type=jnp.float32
    ) + front_decay * jnp.dot(grad_float, entering.T, precision=precise)
    grad_k = jnp.dot(
        dv_weights.T, queries, preferred_element_type=jnp.float32
    ) + tail_decay * jnp.dot(value_rows.astype(jnp.float32), leaving.T, precision=precise)
    grad_v = jnp.dot(
        qk_weights.T, grad_attn, preferred_element_type=jnp.float32
    ) + tail_decay * jnp.dot(key_rows.astype(jnp.float32), leaving, precision=precise)
    arriving = jnp.exp(cumulated[-1]) * leaving + jnp.dot(
        (queries.astype(jnp.float32) * front_decay).T, grad_float, precision=precise
    )
    return (arriving, (grad_q, grad_k, grad_v))


def backward_run(queries, key_rows, value_rows, grad_attn, log_rates, entries, start, block_len):
    pieces = tuple(
        (split_blocks(t, block_len) for t in (queries, key_rows, value_rows, grad_attn, log_rates))
    ) + (entries,)
    closing, (grad_q, grad_k, grad_v) = lax.scan(block_backward, start, pieces, reverse=True)
    shape = queries.shape
    return (grad_q.reshape(shape), grad_k.reshape(shape), grad_v.reshape(shape), closing)


def join_forward(earlier, later_part):
    return (
        jnp.exp(later_part[1])[:, None, None] * earlier[0] + later_part[0],
        earlier[1] + later_part[1],
    )


def join_backward(earlier, later_part):
    return (
        later_part[0] + jnp.exp(later_part[1])[:, None, None] * earlier[0],
        earlier[1] + later_part[1],
    )


def by_heads(tensor, head_count):
    return tensor.reshape(tensor.shape[0], head_count, HEAD_DIM).transpose(1, 0, 2)


def from_heads(tensor):
    return tensor.transpose(1, 0, 2).reshape(tensor.shape[1], tensor.shape[0] * tensor.shape[2])


def on_device(queries, key_rows, value_rows, gate_input, norm_gain, log_decay, grad_output):
    length = queries.shape[0]
    head_count = log_decay.shape[0]
    block_len = min(512, length)
    total_width = head_count * HEAD_DIM * lax.axis_size(("section", "exp"))
    zero_state = jnp.zeros((head_count, HEAD_DIM, HEAD_DIM), jnp.float32)
    zero_totals = jnp.zeros((head_count,), jnp.float32)
    query_heads = by_heads(queries, head_count)
    key_heads = by_heads(key_rows, head_count)
    value_heads = by_heads(value_rows, head_count)
    local_out, entries, local_state = jax.vmap(partial(forward_run, block_len=block_len))(
        query_heads, key_heads, value_heads, log_decay, zero_state
    )
    totals = jnp.sum(log_decay, axis=1)
    cumulated = jnp.cumsum(log_decay, axis=1)
    incoming, passed = entering_2(
        (local_state, totals), "ctx", join_forward, (zero_state, zero_totals), False
    )
    front_decay = jnp.exp(cumulated)[..., None]
    attn_heads = local_out + front_decay * jnp.einsum(
        "hti,hij->htj", query_heads.astype(jnp.float32), incoming, precision=precise
    )
    full_out = from_heads(attn_heads)
    gate_prob = jax.nn.sigmoid(gate_input.astype(jnp.float32))
    grad_float = grad_output.astype(jnp.float32)
    signal = grad_float * gate_prob * norm_gain
    squares, raw_sum = lax.psum(
        (jnp.sum(full_out * full_out, axis=1), jnp.sum(signal * full_out, axis=1)),
        ("section", "exp"),
    )
    inv_rms = lax.rsqrt(squares / total_width + epsilon)
    normed = full_out * inv_rms[:, None]
    along = raw_sum * inv_rms / total_width
    scaled = normed * norm_gain
    layer_out = (scaled * gate_prob).astype(jnp.bfloat16)
    grad_gate = (grad_float * scaled * gate_prob * (1.0 - gate_prob)).astype(jnp.bfloat16)
    grad_attn = (inv_rms[:, None] * (signal - normed * along[:, None])).astype(jnp.bfloat16)
    grad_heads = by_heads(grad_attn, head_count)
    local_q, local_k, local_v, local_back = jax.vmap(partial(backward_run, block_len=block_len))(
        query_heads, key_heads, value_heads, grad_heads, log_decay, entries, zero_state
    )
    later_state, passed_back = entering_2(
        (local_back, totals), "ctx", join_backward, (zero_state, zero_totals), True
    )
    tail_decay = jnp.exp(totals[:, None] - cumulated)[..., None]
    grad_q = local_q + front_decay * jnp.einsum(
        "htj,hij->hti", grad_heads.astype(jnp.float32), incoming, precision=precise
    )
    grad_k = local_k + tail_decay * jnp.einsum(
        "htj,hij->hti", value_heads.astype(jnp.float32), later_state, precision=precise
    )
    grad_v = local_v + tail_decay * jnp.einsum(
        "hti,hij->htj", key_heads.astype(jnp.float32), later_state, precision=precise
    )
    return (
        layer_out,
        from_heads(grad_q).astype(jnp.bfloat16),
        from_heads(grad_k).astype(jnp.bfloat16),
        from_heads(grad_v).astype(jnp.bfloat16),
        grad_gate,
    )


def solution(mesh):
    in_specs = (
        P("ctx", ("section", "exp")),
        P("ctx", ("section", "exp")),
        P("ctx", ("section", "exp")),
        P("ctx", ("section", "exp")),
        P(("section", "exp")),
        P(("section", "exp"), "ctx"),
        P("ctx", ("section", "exp")),
    )
    out_specs = (
        P("ctx", ("section", "exp")),
        P("ctx", ("section", "exp")),
        P("ctx", ("section", "exp")),
        P("ctx", ("section", "exp")),
        P("ctx", ("section", "exp")),
    )
    return jax.shard_map(
        on_device, mesh=mesh, in_specs=in_specs, out_specs=out_specs, check_vma=False
    )
```

profile of v0, /device:TPU:0, one launch (start us, length us, event | category | flops | bytes accessed | tf_op | source)
XLA Modules:
  0.0 89.8 jit_solution(807954294924920336)
XLA Ops:
  0.7 0.6 copy-done.9
  1.7 9.4 %while.64 = (s32[]{:T(128)}, f32[1,128,128]{2,1,0:T(8,128)S(1)}, f32[2,1,512,128]{3,2,1,0:T(8,128)S(1)}, f32[2,1,128,128]{3,2,1,0:T(8,128)S(1)}, f32[2,1,512]{2,...) while((s32[]{:T(128)}, f32[1,128,128]{2,1,0:T(8,128)S(1)}, ...), condition=%wide.region_3.4_spmd.clone, body=%wide.region_0.3_spmd.clone.sunk | while | flops 337527296 | bytes 2981717 | solution.py:66
  11.1 7.2 %all-gather = f32[4,128,128]{2,1,0:T(8,128)S(1)} all-gather(f32[1,128,128]{2,1,0:T(8,128)S(1)} %get-tuple-element.398), channel_id=2, replica_groups=mesh['section'=2,'ctx'=4,'exp'=4] {'ctx'}, dimensions={0}, use_global_device_ids=true | all-gather | bytes 327680 | tf_op jit(solution)/shard_map/all_gather | solution.py:19
  18.3 0.7 copy-done.16
  19.6 0.6 reduce_sum.27
  20.2 1.4 %dynamic-update-slice = f32[4]{0:T(128)S(1)} dynamic-update-slice(f32[4]{0:T(128)S(1)} %broadcast.209, f32[1]{0:T(128)} %bitcast.13, u32[]{:T(128)} %bitcast.14) | dynamic-update-slice | bytes 12
  21.6 7.1 %all-reduce = f32[4]{0:T(128)S(1)} all-reduce(f32[4]{0:T(128)S(1)} %dynamic-update-slice), channel_id=1, replica_groups=mesh['section'=2,'ctx'=4,'exp'=4] {'ctx'}, use_global_device_ids=true, to_apply=%add | all-reduce | flops 4 | bytes 32
  30.2 1.3 %subtract_exponential_fusion.2 = (f32[1024]{0:T(1024)}, f32[1024]{0:T(1024)S(1)}) fusion(f32[]{:T(128)} %reduce_sum.27, f32[1024]{0:T(1024)S(1)} %bitcast.319, f32[1,8,128]{2,1,0:T(8,128)S(1)} %reduce-window.42), kind=kLoop, calls=%fused_computation.160 | loop fusion | flops 2048 | bytes 16388 | tf_op jit(solution)/shard_map/exp | solution.py:172
  31.6 0.8 copy-done.8
  33.1 0.6 multiply_reduce_fusion
  33.7 22.2 %all-reduce.1 = (f32[1024]{0:T(1024)S(1)}, f32[1024]{0:T(1024)S(1)}) all-reduce(f32[1024]{0:T(1024)S(1)} %get-tuple-element.548, f32[1024]{0:T(1024)S(1)} %get-tuple-element.547), channel_id=1, replica_groups=mesh['section'=2,'ctx'=4,'exp'=4] {'section','exp'}, use_global_device_ids=true, to_apply=%region_10.11 | all-reduce | flops 2048 | bytes 16384 | tf_op jit(solution)/shard_map/psum | solution.py:154
  56.0 1.1 %fusion.126 = (bf16[1024,128]{0,1:T(8,128)(2,1)S(1)}, bf16[1024,128]{0,1:T(8,128)(2,1)S(1)}, bf16[1024,128]{0,1:T(8,128)(2,1)}) fusion(bf16[1024,128]{0,1:T(8,128)(2,1)S(1)} %copy.39, f32[1024,128]{0,1:T(8,128)S(1)} %get-tuple-element.620, f32[128]{0:T(128)S(1)} %copy-done.13, f32[1024]{0:T(1024)S(1)} %get-tuple-element.619, ...), kind=kLoop, calls=%fused_computation.149 | loop fusion | flops 2621440 | bytes 1843712 | tf_op jit(solution)/shard_map/convert_element_type | solution.py:163
  57.4 0.9 copy-done.3
  58.3 13.5 %while.65 = (s32[]{:T(128)}, f32[1,128,128]{2,1,0:T(8,128)S(1)}, f32[2,1,512,128]{3,2,1,0:T(8,128)S(1)}, f32[2,1,512,128]{3,2,1,0:T(8,128)S(1)}, f32[2,1,512,128...) while((s32[]{:T(128)}, f32[1,128,128]{2,1,0:T(8,128)S(1)}, ...), condition=%wide.region_16.17_spmd.clone, body=%wide.region_13.16_spmd.clone.sunk | while | flops 742015488 | bytes 6926235 | solution.py:101
  59.6 0.6 slice.76
  63.4 0.6 fusion.212
  66.4 0.6 slice.76
  70.2 0.6 fusion.212
  72.0 7.3 %all-gather.1 = f32[4,128,128]{2,1,0:T(8,128)S(1)} all-gather(f32[1,128,128]{2,1,0:T(8,128)S(1)} %get-tuple-element.403), channel_id=3, replica_groups=mesh['section'=2,'ctx'=4,'exp'=4] {'ctx'}, dimensions={0}, use_global_device_ids=true | all-gather | bytes 327680 | tf_op jit(solution)/shard_map/all_gather | solution.py:19
  79.3 0.7 copy-done.15
  80.0 4.2 %while.63 = (s32[]{:T(128)}, f32[1,128,128]{2,1,0:T(8,128)S(1)}, s32[]{:T(128)}, f32[4,1,128,128]{3,2,1,0:T(8,128)S(1)}, f32[4,1]{0,1:T(1,128)S(1)}, /*index=5*/s32[]{:T(128)}, s32[]{:T(128)}, s32[]{:T(128)}, s32[]{:T(128)}) while((s32[]{:T(128)}, f32[1,128,128]{2,1,0:T(8,128)S(1)}, s32[]{:T(128)}, f32[4,1,128,128]{3,2,1,0:T(8,128)S(1)}, ...), condition=%wide.region_18.19_spmd, body=%wide.region_17.18_spmd.sunk | while | flops 32774 | bytes 196767 | solution.py:28
  80.0 0.7 fusion.178
  80.6 0.7 bitcast_add_fusion.10
  81.4 0.7 fusion.178
  82.0 0.7 bitcast_add_fusion.10
  82.8 0.7 fusion.178
  83.4 0.7 bitcast_add_fusion.10
  84.6 0.8 copy.46
  86.0 0.8 copy.45
  86.9 1.2 %fusion.120 = bf16[1024,128]{1,0:T(8,128)(2,1)} fusion(f32[1024,128]{1,0:T(8,128)S(1)} %bitcast.304, bf16[1024,128]{0,1:T(8,128)(2,1)S(1)} %get-tuple-element.614, f32[1024]{0:T(1024)S(1)} %copy-done.12, f32[1,128,128]{2,1,0:T(8,128)S(1)} %get-tuple-element.399), kind=kOutput, calls=%fused_computation.141 | convolution fusion | flops 201719808 | bytes 1118208 | tf_op jit(solution)/shard_map/htj,hij->hti/dot_general | solution.py:173
  88.1 0.8 copy.44
  88.9 0.8 copy.47
  (121 shorter events, 19.7 us)
Async XLA Ops:
  0.6 0.7 copy-start.9
  0.7 1.0 %copy-start = (bf16[1024,128]{1,0:T(8,128)(2,1)S(1)}, bf16[1024,128]{1,0:T(8,128)(2,1)}, u32[]{:S(2)}) copy-start(bf16[1024,128]{1,0:T(8,128)(2,1)} %param.16) | copy-start | bytes 786436
  0.7 1.0 %copy-start.1 = (bf16[1024,128]{1,0:T(8,128)(2,1)S(1)}, bf16[1024,128]{1,0:T(8,128)(2,1)}, u32[]{:S(2)}) copy-start(bf16[1024,128]{1,0:T(8,128)(2,1)} %param.15) | copy-start | bytes 786436
  1.7 1.1 %copy-start.2 = (bf16[2,1,512,128]{3,2,1,0:T(8,128)(2,1)S(1)}, bf16[2,1,512,128]{3,2,1,0:T(8,128)(2,1)}, u32[]{:S(2)}) copy-start(bf16[2,1,512,128]{3,2,1,0:T(8,128)(2,1)} %get-tuple-element.837) | copy-start | bytes 786436 | tf_op jit(solution)/shard_map/vmap()/while
  6.4 1.1 %copy-start.2 = (bf16[2,1,512,128]{3,2,1,0:T(8,128)(2,1)S(1)}, bf16[2,1,512,128]{3,2,1,0:T(8,128)(2,1)}, u32[]{:S(2)}) copy-start(bf16[2,1,512,128]{3,2,1,0:T(8,128)(2,1)} %get-tuple-element.837) | copy-start | bytes 786436 | tf_op jit(solution)/shard_map/vmap()/while
  18.3 0.7 copy-start.16
  28.7 0.6 copy-start.14
  29.3 2.2 %copy-start.7 = (bf16[1024,128]{1,0:T(8,128)(2,1)S(1)}, bf16[1024,128]{1,0:T(8,128)(2,1)}, u32[]{:S(2)}) copy-start(bf16[1024,128]{1,0:T(8,128)(2,1)} %param.18) | copy-start | bytes 786436
  31.5 1.1 %copy-start.11 = (f32[1024]{0:T(1024)}, f32[1024]{0:T(1024)S(1)}, u32[]{:S(2)}) copy-start(f32[1024]{0:T(1024)S(1)} %get-tuple-element.617) | copy-start | bytes 12292
  31.5 1.0 %copy-start.8 = (bf16[1024,128]{1,0:T(8,128)(2,1)S(1)}, bf16[1024,128]{1,0:T(8,128)(2,1)}, u32[]{:S(2)}) copy-start(bf16[1024,128]{1,0:T(8,128)(2,1)} %param.21) | copy-start | bytes 786436
  32.4 0.7 copy-start.13
  57.3 1.0 %copy-start.3 = (bf16[2,1,512,128]{3,2,1,0:T(8,128)(2,1)S(1)}, bf16[2,1,512,128]{3,2,1,0:T(8,128)(2,1)}, u32[]{:S(2)}) copy-start(bf16[2,1,512,128]{3,2,1,0:T(8,128)(2,1)} %get-tuple-element.938) | copy-start | bytes 786436
  58.3 3.9 %copy-start.5 = (f32[2,1,128,128]{3,2,1,0:T(8,128)}, f32[2,1,128,128]{3,2,1,0:T(8,128)S(1)}, u32[]{:S(2)}) copy-start(f32[2,1,128,128]{3,2,1,0:T(8,128)S(1)} %get-tuple-element.904) | copy-start | bytes 393220 | tf_op jit(solution)/shard_map/vmap()/while
  64.1 0.9 %copy-start.6 = (f32[2,1,128,128]{3,2,1,0:T(8,128)S(1)}, f32[2,1,128,128]{3,2,1,0:T(8,128)}, u32[]{:S(2)}) copy-start(f32[2,1,128,128]{3,2,1,0:T(8,128)} %copy-done.5) | copy-start | bytes 393220 | tf_op jit(solution)/shard_map/vmap()/while
  65.0 3.9 %copy-start.5 = (f32[2,1,128,128]{3,2,1,0:T(8,128)}, f32[2,1,128,128]{3,2,1,0:T(8,128)S(1)}, u32[]{:S(2)}) copy-start(f32[2,1,128,128]{3,2,1,0:T(8,128)S(1)} %get-tuple-element.904) | copy-start | bytes 393220 | tf_op jit(solution)/shard_map/vmap()/while
  70.9 0.9 %copy-start.6 = (f32[2,1,128,128]{3,2,1,0:T(8,128)S(1)}, f32[2,1,128,128]{3,2,1,0:T(8,128)}, u32[]{:S(2)}) copy-start(f32[2,1,128,128]{3,2,1,0:T(8,128)} %copy-done.5) | copy-start | bytes 393220 | tf_op jit(solution)/shard_map/vmap()/while
  79.3 0.7 copy-start.15
  80.0 4.2 %copy-start.10 = (f32[1024]{0:T(1024)S(1)}, f32[1024]{0:T(1024)}, u32[]{:S(2)}) copy-start(f32[1024]{0:T(1024)} %get-tuple-element.616) | copy-start | bytes 12292
  86.0 0.9 copy-start.12
  86.9 1.2 %copy-start.4 = (bf16[1024,128]{0,1:T(8,128)(2,1)S(1)}, bf16[1024,128]{0,1:T(8,128)(2,1)}, u32[]{:S(2)}) copy-start(bf16[1024,128]{0,1:T(8,128)(2,1)} %get-tuple-element.615) | copy-start | bytes 786436
where the time goes:
time: 90.2 us; the launch traced here: 89.8 us
  blocking collectives  43.9 us (49%)
  local copies, waits for them, and re-layouts  20.5 us (23%)
  matrix products  11.1 us (12%)
  other arithmetic  7.83 us (9%)
  loops' own time  5.56 us (6%)
    psum x1, blocking collectives, on_device(): lax.psum((jnp.sum(full_out * full_out, axis=1), jnp.sum(signal * full_out...  22.2 us
    all_gather x2, blocking collectives, entering_2(): gathered = jax.tree.map(lambda a: lax.all_gather(a, axis), part)  14.5 us
    unnamed x38, local copies, waits for them, and re-layouts  10.9 us
    unnamed x1, blocking collectives  7.1 us
    another operation x1, loops' own time, forward_run(): closing, (outputs, entries) = lax.scan(block_forward, start, pieces)  2.81 us
    another operation x1, loops' own time, backward_run(): lax.scan(block_backward, start, pieces, reverse=True)  2.67 us
    slice x4, local copies, waits for them, and re-layouts, block_backward(): cumulated[-1]  2.45 us
    another operation x10, other arithmetic  2.42 us

commit v1 on v0

v1 whole, which is shorter than its diff:
```python
from functools import partial

import jax
import jax.numpy as jnp
from jax import lax
from jax.experimental import pallas as pl
from jax.experimental.pallas import tpu as pltpu
from jax.sharding import PartitionSpec as P

MESH = pl.DeviceIdType.MESH
BF = jnp.bfloat16
F32 = jnp.float32
epsilon = 1e-06
EXTRA = 8

NN = (((1,), (0,)), ((), ()))
NT = (((1,), (1,)), ((), ()))
TN = (((0,), (0,)), ((), ()))


def mm(a, b, dims):
    return lax.dot_general(a, b, dims, preferred_element_type=F32)


def split(x):
    high = x.astype(BF)
    return high, (x - high.astype(F32)).astype(BF)


def prefix_rows(x):
    lane = lax.broadcasted_iota(jnp.int32, x.shape, 1)
    shift = 1
    while shift < x.shape[1]:
        x = x + jnp.where(lane >= shift, pltpu.roll(x, shift, 1), 0.0)
        shift *= 2
    return x


def kernel(
    sizes,
    q_h, k_h, v_h, gi_h, go_h, gain_ref, ld_ref,
    lo_h, gq_h, gk_h, gv_h, gg_h,
    q, k, v, gi, go, lo, gq, gk, gv, gg,
    steps, fd, tail, table, wq, attn, signal, gate, upd, ent, g, gkl, gvl,
    fsend, frecv, bsend, brecv, acc, rsend, rrecv, coef,
    in_sem, out_sem, fs_sem, fr_sem, bs_sem, br_sem, rs_sem, rr_sem,
):
    n_ctx, n_sec, n_exp, chunk = sizes
    n_norm = n_sec * n_exp
    length, dim = q.shape
    count = length // chunk
    me = lax.axis_index("ctx")
    sec = lax.axis_index("section")
    ex = lax.axis_index("exp")
    mine = sec * n_exp + ex
    width = float(dim * n_norm)

    def norm_peer(r):
        other = lax.rem(mine + r, n_norm)
        return {"section": lax.div(other, n_exp), "exp": lax.rem(other, n_exp)}

    barrier = pltpu.get_barrier_semaphore()
    for r in range(1, n_ctx):
        pl.semaphore_signal(
            barrier, inc=1, device_id={"ctx": lax.rem(me + r, n_ctx)}, device_id_type=MESH
        )
    for r in range(1, n_norm):
        pl.semaphore_signal(barrier, inc=1, device_id=norm_peer(r), device_id_type=MESH)

    loads = [
        pltpu.make_async_copy(src, dst, in_sem.at[i])
        for i, (src, dst) in enumerate(
            ((k_h, k), (v_h, v), (q_h, q), (gi_h, gi), (go_h, go))
        )
    ]
    for copy in loads:
        copy.start()
    stores = [
        pltpu.make_async_copy(src, dst, out_sem.at[i])
        for i, (src, dst) in enumerate(
            ((lo, lo_h), (gg, gg_h), (gq, gq_h), (gk, gk_h), (gv, gv_h))
        )
    ]

    rows = [pl.ds(c * chunk, chunk) for c in range(count)]

    steps[...] = jnp.zeros_like(steps)
    for c in range(count):
        steps[c : c + 1, :] = ld_ref[:, c * chunk : (c + 1) * chunk]
    run = prefix_rows(steps[...])
    steps[...] = run
    run_t = jnp.transpose(run)
    ends = [run[c : c + 1, chunk - 1 : chunk] for c in range(count)]
    for c in range(count):
        column = jnp.broadcast_to(run_t[:, c : c + 1], (chunk, dim))
        fd[rows[c], :] = jnp.exp(column)
        tail[rows[c], :] = jnp.exp(ends[c] - column)

    loads[0].wait()
    loads[1].wait()
    local = None
    total = None
    for c in range(count):
        high, low = split(k[rows[c], :].astype(F32) * tail[rows[c], :])
        vc = v[rows[c], :]
        update = mm(high, vc, TN) + mm(low, vc, TN)
        upd[c] = update
        local = update if local is None else jnp.exp(ends[c]) * local + update
        total = ends[c] if total is None else total + ends[c]
    fsend[0:dim, :] = local
    fsend[dim : dim + EXTRA, :] = jnp.broadcast_to(total, (EXTRA, dim))

    pl.semaphore_wait(barrier, n_ctx - 1 + n_norm - 1)

    def forward_copy(r):
        return pltpu.make_async_remote_copy(
            src_ref=fsend, dst_ref=frecv.at[r], send_sem=fs_sem.at[r], recv_sem=fr_sem.at[r],
            device_id={"ctx": lax.rem(me + r, n_ctx)}, device_id_type=MESH,
        )

    def backward_copy(r):
        return pltpu.make_async_remote_copy(
            src_ref=bsend, dst_ref=brecv.at[r], send_sem=bs_sem.at[r], recv_sem=br_sem.at[r],
            device_id={"ctx": lax.rem(me + n_ctx - r, n_ctx)}, device_id_type=MESH,
        )

    def row_copy(r):
        return pltpu.make_async_remote_copy(
            src_ref=rsend, dst_ref=rrecv.at[r], send_sem=rs_sem.at[r], recv_sem=rr_sem.at[r],
            device_id=norm_peer(r), device_id_type=MESH,
        )

    for r in range(1, n_ctx):
        @pl.when(me + r < n_ctx)
        def _(r=r):
            forward_copy(r).start()

    loads[2].wait()
    t_index = lax.broadcasted_iota(jnp.int32, (chunk, chunk), 0)
    s_index = lax.broadcasted_iota(jnp.int32, (chunk, chunk), 1)
    for c in range(count):
        column = jnp.broadcast_to(run_t[:, c : c + 1], (chunk, chunk))
        gap = jnp.minimum(column - steps[c : c + 1, :], 0.0)
        weights = jnp.where(t_index >= s_index, jnp.exp(gap), 0.0)
        table[c] = weights
        scores = (mm(q[rows[c], :], k[rows[c], :], NT) * weights).astype(BF)
        wq[c] = scores
        attn[rows[c], :] = mm(scores, v[rows[c], :], NN)
    loads[3].wait()
    loads[4].wait()
    gain = gain_ref[...]
    for c in range(count):
        prob = jax.nn.sigmoid(gi[rows[c], :].astype(F32))
        gate[rows[c], :] = prob
        signal[rows[c], :] = go[rows[c], :].astype(F32) * prob * gain

    acc[...] = jnp.zeros_like(acc)
    for r in range(n_ctx - 1, 0, -1):
        @pl.when(me >= r)
        def _(r=r):
            forward_copy(r).wait_recv()
            acc[...] = jnp.exp(frecv[r, dim : dim + 1, :]) * acc[...] + frecv[r, 0:dim, :]

    state = acc[...]
    ones = jnp.ones((8, dim), BF)
    for c in range(count):
        high, low = split(state)
        ent[c, :, 0:dim] = high
        ent[c, :, dim : 2 * dim] = low
        both = mm(q[rows[c], :], ent[c], NN)
        full = attn[rows[c], :] + fd[rows[c], :] * (both[:, 0:dim] + both[:, dim : 2 * dim])
        attn[rows[c], :] = full
        rsend[0:1, rows[c]] = mm(ones, (full * full).astype(BF), NT)[0:1, :]
        rsend[1:2, rows[c]] = mm(ones, (signal[rows[c], :] * full).astype(BF), NT)[0:1, :]
        if c + 1 < count:
            state = jnp.exp(ends[c]) * state + upd[c]

    for r in range(1, n_norm):
        row_copy(r).start()
    coef[...] = jnp.zeros_like(coef)
    sums = rsend[...]
    for r in range(1, n_norm):
        row_copy(r).wait_recv()
        sums = sums + rrecv[r]
    inv = lax.rsqrt(sums[0:1, :] / width + epsilon)
    coef[0:1, :] = inv
    coef[1:2, :] = inv * inv * (sums[1:2, :] / width)

    seen = [None] * count
    for c in range(count):
        turned = jnp.transpose(coef[:, rows[c]])
        inv_b = jnp.broadcast_to(turned[:, 0:1], (chunk, dim))
        along_b = jnp.broadcast_to(turned[:, 1:2], (chunk, dim))
        full = attn[rows[c], :]
        grad = (inv_b * (signal[rows[c], :] - full * along_b)).astype(BF)
        g[rows[c], :] = grad
        high, low = split(q[rows[c], :].astype(F32) * fd[rows[c], :])
        seen[c] = mm(high, grad, TN) + mm(low, grad, TN)
        upd[c] = seen[c]
        scaled = full * inv_b * gain
        prob = gate[rows[c], :]
        out = scaled * prob
        lo[rows[c], :] = out.astype(BF)
        gg[rows[c], :] = (go[rows[c], :].astype(F32) * out * (1.0 - prob)).astype(BF)
    local = None
    for c in range(count - 1, -1, -1):
        local = seen[c] if local is None else jnp.exp(ends[c]) * local + seen[c]
    bsend[0:dim, :] = local
    bsend[dim : dim + EXTRA, :] = jnp.broadcast_to(total, (EXTRA, dim))
    for r in range(1, n_ctx):
        @pl.when(me >= r)
        def _(r=r):
            backward_copy(r).start()
    stores[0].start()
    stores[1].start()

    for c in range(count):
        grad = g[rows[c], :]
        dv = (mm(grad, v[rows[c], :], NT) * table[c]).astype(BF)
        high = mm(grad, ent[c, :, 0:dim], NT)
        low = mm(grad, ent[c, :, dim : 2 * dim], NT)
        gq[rows[c], :] = (
            mm(dv, k[rows[c], :], NN) + fd[rows[c], :] * (high + low)
        ).astype(BF)
        gkl[rows[c], :] = mm(dv, q[rows[c], :], TN)
        gvl[rows[c], :] = mm(wq[c], grad, TN)
    stores[2].start()

    acc[...] = jnp.zeros_like(acc)
    for r in range(n_ctx - 1, 0, -1):
        @pl.when(me + r < n_ctx)
        def _(r=r):
            backward_copy(r).wait_recv()
            acc[...] = jnp.exp(brecv[r, dim : dim + 1, :]) * acc[...] + brecv[r, 0:dim, :]

    state = acc[...]
    for c in range(count - 1, -1, -1):
        high, low = split(state)
        fall = tail[rows[c], :]
        vc = v[rows[c], :]
        kc = k[rows[c], :]
        gk[rows[c], :] = (gkl[rows[c], :] + fall * (mm(vc, high, NT) + mm(vc, low, NT))).astype(BF)
        gv[rows[c], :] = (gvl[rows[c], :] + fall * (mm(kc, high, NN) + mm(kc, low, NN))).astype(BF)
        if c > 0:
            state = jnp.exp(ends[c]) * state + upd[c]
    stores[3].start()
    stores[4].start()

    for r in range(1, n_ctx):
        @pl.when(me + r < n_ctx)
        def _(r=r):
            forward_copy(r).wait_send()

        @pl.when(me >= r)
        def _(r=r):
            backward_copy(r).wait_send()
    for r in range(1, n_norm):
        row_copy(r).wait_send()
    for copy in stores:
        copy.wait()


def on_device(n_ctx, n_sec, n_exp, queries, key_rows, value_rows, gate_input, norm_gain, log_decay, grad_output):
    length, dim = queries.shape
    assert log_decay.shape[0] == 1
    chunk = min(256, length)
    count = length // chunk
    assert count * chunk == length and count <= 8
    n_norm = n_sec * n_exp
    any_spec = pl.BlockSpec(memory_space=pl.ANY)
    vmem_spec = pl.BlockSpec(memory_space=pltpu.VMEM)
    block = lambda dtype: pltpu.VMEM((length, dim), dtype)
    sem = lambda n: pltpu.SemaphoreType.DMA((n,))
    return pl.pallas_call(
        partial(kernel, (n_ctx, n_sec, n_exp, chunk)),
        out_shape=[jax.ShapeDtypeStruct((length, dim), BF)] * 5,
        in_specs=[any_spec] * 5 + [vmem_spec] * 2,
        out_specs=[any_spec] * 5,
        scratch_shapes=[block(BF)] * 10
        + [
            pltpu.VMEM((8, chunk), F32),
            block(F32),
            block(F32),
            pltpu.VMEM((count, chunk, chunk), F32),
            pltpu.VMEM((count, chunk, chunk), BF),
            block(F32),
            block(F32),
            block(F32),
            pltpu.VMEM((count, dim, dim), F32),
            pltpu.VMEM((count, dim, 2 * dim), BF),
            block(BF),
            block(F32),
            block(F32),
            pltpu.VMEM((dim + EXTRA, dim), F32),
            pltpu.VMEM((n_ctx, dim + EXTRA, dim), F32),
            pltpu.VMEM((dim + EXTRA, dim), F32),
            pltpu.VMEM((n_ctx, dim + EXTRA, dim), F32),
            pltpu.VMEM((dim, dim), F32),
            pltpu.VMEM((2, length), F32),
            pltpu.VMEM((n_norm, 2, length), F32),
            pltpu.VMEM((8, length), F32),
            sem(5), sem(5), sem(n_ctx), sem(n_ctx), sem(n_ctx), sem(n_ctx), sem(n_norm), sem(n_norm),
        ],
        compiler_params=pltpu.CompilerParams(
            collective_id=0, has_side_effects=True, vmem_limit_bytes=48 * 1024 * 1024
        ),
    )(queries, key_rows, value_rows, gate_input, grad_output, norm_gain.reshape(1, dim), log_decay)


def solution(mesh):
    rows = P("ctx", ("section", "exp"))
    in_specs = (rows, rows, rows, rows, P(("section", "exp")), P(("section", "exp"), "ctx"), rows)
    call = partial(on_device, mesh.shape["ctx"], mesh.shape["section"], mesh.shape["exp"])

    def run(*args):
        return tuple(call(*args))

    return jax.shard_map(run, mesh=mesh, in_specs=in_specs, out_specs=(rows,) * 5, check_vma=False)
```

time: 90.2 us -> 31.6 us (0.35)
  blocking collectives: 43.9 us -> 0 us
  Pallas kernels: 0 us -> 21 us
  matrix products: 11.1 us -> 0 us
  local copies, waits for them, and re-layouts: 20.5 us -> 9.6 us
  other arithmetic: 7.83 us -> 0 us
  loops' own time: 5.56 us -> 0 us
    psum x1 -> x0, blocking collectives: 22.2 us -> none  [on_device(): lax.psum((jnp.sum(full_out * full_out, axis=1), jnp.sum(signal * full_out...]
    pallas_call x0 -> x1, Pallas kernels: none -> 21 us  [on_device(): pl.pallas_call(partial(kernel, (n_ctx, n_sec, n_exp, chunk)), out_shape=[...]
    all_gather x2 -> x0, blocking collectives: 14.5 us -> none  [entering_2(): gathered = jax.tree.map(lambda a: lax.all_gather(a, axis), part)]
    dot_general x26 -> x0, matrix products: 11.1 us -> none  [the longest x2 1.26 us: block_backward(): jnp.dot(qk_weights.T, grad_attn, preferred_element_type=jnp.float32)]
    unnamed x1 -> x0, blocking collectives: 7.1 us -> none
    another operation x4 -> x0, loops' own time: 5.56 us -> none  [the longest x1 2.81 us: forward_run(): closing, (outputs, entries) = lax.scan(block_forward, start, pieces)]
    slice x10 -> x0, local copies, waits for them, and re-layouts: 5.15 us -> none  [the longest x4 2.45 us: block_backward(): cumulated[-1]]
    another operation x10 -> x0, other arithmetic: 2.42 us -> none
where the time goes in v1:
time: 31.6 us; the launch traced here: 31.2 us
  Pallas kernels  21 us (66%)
  local copies, waits for them, and re-layouts  9.6 us (30%)
  between operations  0.66 us (2%)
    pallas_call x1, Pallas kernels, on_device(): pl.pallas_call(partial(kernel, (n_ctx, n_sec, n_exp, chunk)), out_shape=[...  21 us
    unnamed x19, local copies, waits for them, and re-layouts  9.6 us

profile of v1, /device:TPU:0, one launch (start us, length us, event | category | flops | bytes accessed | tf_op | source)
XLA Modules:
  0.0 31.2 jit_solution(4107954063642530027)
XLA Ops:
  0.6 0.0 copy-start.6
  0.6 0.6 %copy-done.6 = f32[128]{0:T(128)S(1)} copy-done((f32[128]{0:T(128)S(1)}, f32[128]{0:T(128)}, u32[]{:S(2)}) %copy-start.6) | copy-done | bytes 536
  1.3 0.0 copy-start
  1.3 0.9 %copy-done = bf16[1024,128]{1,0:T(8,128)(2,1)S(1)} copy-done((bf16[1024,128]{1,0:T(8,128)(2,1)S(1)}, bf16[1024,128]{1,0:T(8,128)(2,1)}, u32[]{:S(2)}) %copy-start) | copy-done | bytes 262168
  2.2 0.0 copy-start.1
  2.2 0.9 %copy-done.1 = bf16[1024,128]{1,0:T(8,128)(2,1)S(1)} copy-done((bf16[1024,128]{1,0:T(8,128)(2,1)S(1)}, bf16[1024,128]{1,0:T(8,128)(2,1)}, u32[]{:S(2)}) %copy-start.1) | copy-done | bytes 262168
  3.2 0.0 copy-start.2
  3.2 0.9 %copy-done.2 = bf16[1024,128]{1,0:T(8,128)(2,1)S(1)} copy-done((bf16[1024,128]{1,0:T(8,128)(2,1)S(1)}, bf16[1024,128]{1,0:T(8,128)(2,1)}, u32[]{:S(2)}) %copy-start.2) | copy-done | bytes 262168
  4.1 0.0 copy-start.3
  4.1 0.9 %copy-done.3 = bf16[1024,128]{1,0:T(8,128)(2,1)S(1)} copy-done((bf16[1024,128]{1,0:T(8,128)(2,1)S(1)}, bf16[1024,128]{1,0:T(8,128)(2,1)}, u32[]{:S(2)}) %copy-start.3) | copy-done | bytes 262168
  5.1 0.0 copy-start.4
  5.1 0.9 %copy-done.4 = bf16[1024,128]{1,0:T(8,128)(2,1)S(1)} copy-done((bf16[1024,128]{1,0:T(8,128)(2,1)S(1)}, bf16[1024,128]{1,0:T(8,128)(2,1)}, u32[]{:S(2)}) %copy-start.4) | copy-done | bytes 262168
  6.0 0.0 copy-start.5
  6.0 0.7 %copy-done.5 = f32[1,1024]{1,0:T(1,128)S(1)} copy-done((f32[1,1024]{1,0:T(1,128)S(1)}, f32[1,1024]{1,0:T(1,128)}, u32[]{:S(2)}) %copy-start.5) | copy-done | bytes 4120
  6.7 21.0 %shard_map.110 = (bf16[1024,128]{1,0:T(8,128)(2,1)S(1)}, bf16[1024,128]{1,0:T(8,128)(2,1)S(1)}, bf16[1024,128]{1,0:T(8,128)(2,1)S(1)}, bf16[1024,128]{1,0:T(8,128)(2,1)S(1)}, bf16[1024,128]{1,0:T(8,128)(2,1)S(1)}) custom-call(bf16[1024,128]{1,0:T(8,128)(2,1)S(1)} %copy-done, bf16[1024,128]{1,0:T(8,128)(2,1)S(1)} %copy-done.1, ...), custom_call_target="tpu_custom_call" | custom-call | tf_op jit(solution)/shard_map/pallas_call | solution.py:274
  27.7 0.7 %copy.17 = bf16[1024,128]{1,0:T(8,128)(2,1)} copy(bf16[1024,128]{1,0:T(8,128)(2,1)S(1)} %get-tuple-element.10) | data formatting | bytes 524288
  28.4 0.7 %copy.18 = bf16[1024,128]{1,0:T(8,128)(2,1)} copy(bf16[1024,128]{1,0:T(8,128)(2,1)S(1)} %get-tuple-element.11) | data formatting | bytes 524288
  29.1 0.7 %copy.19 = bf16[1024,128]{1,0:T(8,128)(2,1)} copy(bf16[1024,128]{1,0:T(8,128)(2,1)S(1)} %get-tuple-element.12) | data formatting | bytes 524288
  29.8 0.7 %copy.20 = bf16[1024,128]{1,0:T(8,128)(2,1)} copy(bf16[1024,128]{1,0:T(8,128)(2,1)S(1)} %get-tuple-element.13) | data formatting | bytes 524288
  30.5 0.7 %copy.21 = bf16[1024,128]{1,0:T(8,128)(2,1)} copy(bf16[1024,128]{1,0:T(8,128)(2,1)S(1)} %get-tuple-element.14) | data formatting | bytes 524288
Async XLA Ops:
  0.6 0.7 %copy-start.6 = (f32[128]{0:T(128)S(1)}, f32[128]{0:T(128)}, u32[]{:S(2)}) copy-start(f32[128]{0:T(128)} %param.11) | copy-start | bytes 1540
  1.3 0.9 %copy-start = (bf16[1024,128]{1,0:T(8,128)(2,1)S(1)}, bf16[1024,128]{1,0:T(8,128)(2,1)}, u32[]{:S(2)}) copy-start(bf16[1024,128]{1,0:T(8,128)(2,1)} %q_h.1) | copy-start | bytes 786436
  2.2 0.9 %copy-start.1 = (bf16[1024,128]{1,0:T(8,128)(2,1)S(1)}, bf16[1024,128]{1,0:T(8,128)(2,1)}, u32[]{:S(2)}) copy-start(bf16[1024,128]{1,0:T(8,128)(2,1)} %k_h.1) | copy-start | bytes 786436
  3.2 0.9 %copy-start.2 = (bf16[1024,128]{1,0:T(8,128)(2,1)S(1)}, bf16[1024,128]{1,0:T(8,128)(2,1)}, u32[]{:S(2)}) copy-start(bf16[1024,128]{1,0:T(8,128)(2,1)} %v_h.1) | copy-start | bytes 786436
  4.1 0.9 %copy-start.3 = (bf16[1024,128]{1,0:T(8,128)(2,1)S(1)}, bf16[1024,128]{1,0:T(8,128)(2,1)}, u32[]{:S(2)}) copy-start(bf16[1024,128]{1,0:T(8,128)(2,1)} %gi_h.1) | copy-start | bytes 786436
  5.1 0.9 %copy-start.4 = (bf16[1024,128]{1,0:T(8,128)(2,1)S(1)}, bf16[1024,128]{1,0:T(8,128)(2,1)}, u32[]{:S(2)}) copy-start(bf16[1024,128]{1,0:T(8,128)(2,1)} %go_h.1) | copy-start | bytes 786436
  6.0 0.7 %copy-start.5 = (f32[1,1024]{1,0:T(1,128)S(1)}, f32[1,1024]{1,0:T(1,128)}, u32[]{:S(2)}) copy-start(f32[1,1024]{1,0:T(1,128)} %ld_ref.1) | copy-start | bytes 12292

commit v2 on v1

--- a/solution.py
+++ b/solution.py
@@ -38,10 +38,10 @@
 
 def kernel(
     sizes,
-    q_h, k_h, v_h, gi_h, go_h, gain_ref, ld_ref,
+    q_h, k_h, v_h, gi_h, go_h, gain_h, ld_h,
     lo_h, gq_h, gk_h, gv_h, gg_h,
     q, k, v, gi, go, lo, gq, gk, gv, gg,
-    steps, fd, tail, table, wq, attn, signal, gate, upd, ent, g, gkl, gvl,
+    gain_ref, ld_ref, steps, fd, tail, table, wq, attn, signal, gate, upd, ent, g, gkl, gvl,
     fsend, frecv, bsend, brecv, acc, rsend, rrecv, coef,
     in_sem, out_sem, fs_sem, fr_sem, bs_sem, br_sem, rs_sem, rr_sem,
 ):
@@ -59,6 +59,15 @@
         other = lax.rem(mine + r, n_norm)
         return {"section": lax.div(other, n_exp), "exp": lax.rem(other, n_exp)}
 
+    loads = [
+        pltpu.make_async_copy(src, dst, in_sem.at[i])
+        for i, (src, dst) in enumerate(
+            ((k_h, k), (v_h, v), (q_h, q), (gi_h, gi), (go_h, go), (gain_h, gain_ref), (ld_h, ld_ref))
+        )
+    ]
+    for i in (6, 0, 1, 2, 3, 4, 5):
+        loads[i].start()
+
     barrier = pltpu.get_barrier_semaphore()
     for r in range(1, n_ctx):
         pl.semaphore_signal(
@@ -67,14 +76,6 @@
     for r in range(1, n_norm):
         pl.semaphore_signal(barrier, inc=1, device_id=norm_peer(r), device_id_type=MESH)
 
-    loads = [
-        pltpu.make_async_copy(src, dst, in_sem.at[i])
-        for i, (src, dst) in enumerate(
-            ((k_h, k), (v_h, v), (q_h, q), (gi_h, gi), (go_h, go))
-        )
-    ]
-    for copy in loads:
-        copy.start()
     stores = [
         pltpu.make_async_copy(src, dst, out_sem.at[i])
         for i, (src, dst) in enumerate(
@@ -85,6 +86,7 @@
     rows = [pl.ds(c * chunk, chunk) for c in range(count)]
 
     steps[...] = jnp.zeros_like(steps)
+    loads[6].wait()
     for c in range(count):
         steps[c : c + 1, :] = ld_ref[:, c * chunk : (c + 1) * chunk]
     run = prefix_rows(steps[...])
@@ -148,6 +150,7 @@
         attn[rows[c], :] = mm(scores, v[rows[c], :], NN)
     loads[3].wait()
     loads[4].wait()
+    loads[5].wait()
     gain = gain_ref[...]
     for c in range(count):
         prob = jax.nn.sigmoid(gi[rows[c], :].astype(F32))
@@ -260,6 +263,14 @@
         copy.wait()
 
 
+def hand_out(*refs):
+    copies = [pltpu.make_async_copy(refs[i], refs[5 + i], refs[10].at[i]) for i in range(5)]
+    for copy in copies:
+        copy.start()
+    for copy in copies:
+        copy.wait()
+
+
 def on_device(n_ctx, n_sec, n_exp, queries, key_rows, value_rows, gate_input, norm_gain, log_decay, grad_output):
     length, dim = queries.shape
     assert log_decay.shape[0] == 1
@@ -268,16 +279,18 @@
     assert count * chunk == length and count <= 8
     n_norm = n_sec * n_exp
     any_spec = pl.BlockSpec(memory_space=pl.ANY)
-    vmem_spec = pl.BlockSpec(memory_space=pltpu.VMEM)
+    hbm_spec = pl.BlockSpec(memory_space=pltpu.HBM)
     block = lambda dtype: pltpu.VMEM((length, dim), dtype)
     sem = lambda n: pltpu.SemaphoreType.DMA((n,))
-    return pl.pallas_call(
+    results = pl.pallas_call(
         partial(kernel, (n_ctx, n_sec, n_exp, chunk)),
         out_shape=[jax.ShapeDtypeStruct((length, dim), BF)] * 5,
-        in_specs=[any_spec] * 5 + [vmem_spec] * 2,
+        in_specs=[hbm_spec] * 7,
         out_specs=[any_spec] * 5,
         scratch_shapes=[block(BF)] * 10
         + [
+            pltpu.VMEM((1, dim), F32),
+            pltpu.VMEM((1, length), F32),
             pltpu.VMEM((8, chunk), F32),
             block(F32),
             block(F32),
@@ -299,12 +312,22 @@
             pltpu.VMEM((2, length), F32),
             pltpu.VMEM((n_norm, 2, length), F32),
             pltpu.VMEM((8, length), F32),
-            sem(5), sem(5), sem(n_ctx), sem(n_ctx), sem(n_ctx), sem(n_ctx), sem(n_norm), sem(n_norm),
+            sem(7), sem(5), sem(n_ctx), sem(n_ctx), sem(n_ctx), sem(n_ctx), sem(n_norm), sem(n_norm),
         ],
         compiler_params=pltpu.CompilerParams(
             collective_id=0, has_side_effects=True, vmem_limit_bytes=48 * 1024 * 1024
         ),
-    )(queries, key_rows, value_rows, gate_input, grad_output, norm_gain.reshape(1, dim), log_decay)
+    )(*[
+        pltpu.with_memory_space_constraint(x, pltpu.HBM)
+        for x in (queries, key_rows, value_rows, gate_input, grad_output, norm_gain.reshape(1, dim), log_decay)
+    ])
+    return pl.pallas_call(
+        hand_out,
+        out_shape=[jax.ShapeDtypeStruct((length, dim), BF)] * 5,
+        in_specs=[any_spec] * 5,
+        out_specs=[hbm_spec] * 5,
+        scratch_shapes=[sem(5)],
+    )(*results)
 
 
 def solution(mesh):

time: 31.6 us -> 66.1 us (2.09)
  Pallas kernels: 21 us -> 61.8 us
  local copies, waits for them, and re-layouts: 9.6 us -> 3.47 us
    pallas_call x0 -> x1, Pallas kernels: none -> 40.8 us  [on_device(): pl.pallas_call(hand_out, out_shape=[jax.ShapeDtypeStruct((length, dim), B...]
    unnamed x19 -> x10, local copies, waits for them, and re-layouts: 9.6 us -> 3.47 us
where the time goes in v2:
time: 66.1 us; the launch traced here: 65.9 us
  Pallas kernels  61.8 us (93%)
  local copies, waits for them, and re-layouts  3.47 us (5%)
    pallas_call x1, Pallas kernels, on_device(): pl.pallas_call(hand_out, out_shape=[jax.ShapeDtypeStruct((length, dim), B...  40.8 us
    pallas_call x1, Pallas kernels, on_device(): pl.pallas_call(partial(kernel, (n_ctx, n_sec, n_exp, chunk)), out_shape=[...  20.9 us
    unnamed x10, local copies, waits for them, and re-layouts  3.47 us

profile of v2, /device:TPU:0, one launch (start us, length us, event | category | flops | bytes accessed | tf_op | source)
XLA Modules:
  0.0 65.9 jit_solution(10360187958957010900)
XLA Ops:
  0.6 20.9 %shard_map.110 = (bf16[1024,128]{1,0:T(8,128)(2,1)S(1)}, bf16[1024,128]{1,0:T(8,128)(2,1)S(1)}, bf16[1024,128]{1,0:T(8,128)(2,1)S(1)}, bf16[1024,128]{1,0:T(8,128)(2,1)S(1)}, bf16[1024,128]{1,0:T(8,128)(2,1)S(1)}) custom-call(bf16[1024,128]{1,0:T(8,128)(2,1)} %q_h.1, bf16[1024,128]{1,0:T(8,128)(2,1)} %k_h.1, bf16[1024,128]{1,0:T(8,128)(2,1)} %v_h.1, ...), custom_call_target="tpu_custom_call" | custom-call | tf_op jit(solution)/shard_map/pallas_call | solution.py:285
  21.6 0.0 copy-start
  21.6 0.7 %copy-done = bf16[1024,128]{1,0:T(8,128)(2,1)} copy-done((bf16[1024,128]{1,0:T(8,128)(2,1)}, bf16[1024,128]{1,0:T(8,128)(2,1)S(1)}, u32[]{:S(2)}) %copy-start) | copy-done | bytes 262168
  22.3 0.0 copy-start.1
  22.3 0.7 %copy-done.1 = bf16[1024,128]{1,0:T(8,128)(2,1)} copy-done((bf16[1024,128]{1,0:T(8,128)(2,1)}, bf16[1024,128]{1,0:T(8,128)(2,1)S(1)}, u32[]{:S(2)}) %copy-start.1) | copy-done | bytes 262168
  23.0 0.0 copy-start.2
  23.0 0.7 %copy-done.2 = bf16[1024,128]{1,0:T(8,128)(2,1)} copy-done((bf16[1024,128]{1,0:T(8,128)(2,1)}, bf16[1024,128]{1,0:T(8,128)(2,1)S(1)}, u32[]{:S(2)}) %copy-start.2) | copy-done | bytes 262168
  23.7 0.0 copy-start.3
  23.7 0.7 %copy-done.3 = bf16[1024,128]{1,0:T(8,128)(2,1)} copy-done((bf16[1024,128]{1,0:T(8,128)(2,1)}, bf16[1024,128]{1,0:T(8,128)(2,1)S(1)}, u32[]{:S(2)}) %copy-start.3) | copy-done | bytes 262168
  24.4 0.0 copy-start.4
  24.4 0.7 %copy-done.4 = bf16[1024,128]{1,0:T(8,128)(2,1)} copy-done((bf16[1024,128]{1,0:T(8,128)(2,1)}, bf16[1024,128]{1,0:T(8,128)(2,1)S(1)}, u32[]{:S(2)}) %copy-start.4) | copy-done | bytes 262168
  25.1 40.8 %shard_map.111 = (bf16[1024,128]{1,0:T(8,128)(2,1)}, bf16[1024,128]{1,0:T(8,128)(2,1)}, bf16[1024,128]{1,0:T(8,128)(2,1)}, bf16[1024,128]{1,0:T(8,128)(2,1)}, bf16[1024,128]{1,0:T(8,128)(2,1)}) custom-call(bf16[1024,128]{1,0:T(8,128)(2,1)} %copy-done, bf16[1024,128]{1,0:T(8,128)(2,1)} %copy-done.1, bf16[1024,128]{1,0:T(8,128)(2,1)} %copy-done.2, ...), custom_call_target="tpu_custom_call" | custom-call | tf_op jit(solution)/shard_map/pallas_call | solution.py:324
Async XLA Ops:
  21.6 0.7 %copy-start = (bf16[1024,128]{1,0:T(8,128)(2,1)}, bf16[1024,128]{1,0:T(8,128)(2,1)S(1)}, u32[]{:S(2)}) copy-start(bf16[1024,128]{1,0:T(8,128)(2,1)S(1)} %get-tuple-element.10.refs_0_) | copy-start | bytes 786436
  22.3 0.7 %copy-start.1 = (bf16[1024,128]{1,0:T(8,128)(2,1)}, bf16[1024,128]{1,0:T(8,128)(2,1)S(1)}, u32[]{:S(2)}) copy-start(bf16[1024,128]{1,0:T(8,128)(2,1)S(1)} %get-tuple-element.11.refs_1_) | copy-start | bytes 786436
  23.0 0.7 %copy-start.2 = (bf16[1024,128]{1,0:T(8,128)(2,1)}, bf16[1024,128]{1,0:T(8,128)(2,1)S(1)}, u32[]{:S(2)}) copy-start(bf16[1024,128]{1,0:T(8,128)(2,1)S(1)} %get-tuple-element.12.refs_2_) | copy-start | bytes 786436
  23.7 0.7 %copy-start.3 = (bf16[1024,128]{1,0:T(8,128)(2,1)}, bf16[1024,128]{1,0:T(8,128)(2,1)S(1)}, u32[]{:S(2)}) copy-start(bf16[1024,128]{1,0:T(8,128)(2,1)S(1)} %get-tuple-element.13.refs_3_) | copy-start | bytes 786436
  24.4 0.7 %copy-start.4 = (bf16[1024,128]{1,0:T(8,128)(2,1)}, bf16[1024,128]{1,0:T(8,128)(2,1)S(1)}, u32[]{:S(2)}) copy-start(bf16[1024,128]{1,0:T(8,128)(2,1)S(1)} %get-tuple-element.14.refs_4_) | copy-start | bytes 786436

commit v3 on v2

--- a/solution.py
+++ b/solution.py
@@ -327,7 +327,8 @@
         in_specs=[any_spec] * 5,
         out_specs=[hbm_spec] * 5,
         scratch_shapes=[sem(5)],
-    )(*results)
+        compiler_params=pltpu.CompilerParams(vmem_limit_bytes=2 * 1024 * 1024),
+    )(*[pltpu.with_memory_space_constraint(x, pltpu.VMEM) for x in results])
 
 
 def solution(mesh):

time: 66.1 us -> 22.9 us (0.35)
  Pallas kernels: 61.8 us -> 22 us
  local copies, waits for them, and re-layouts: 3.47 us -> 0 us
    pallas_call x1, Pallas kernels: 40.8 us -> 1.09 us  [on_device(): pl.pallas_call(hand_out, out_shape=[jax.ShapeDtypeStruct((length, dim), B...]
    unnamed x10 -> x0, local copies, waits for them, and re-layouts: 3.47 us -> none
where the time goes in v3:
time: 22.9 us; the launch traced here: 22.7 us
  Pallas kernels  22 us (96%)
  between operations  0.64 us (3%)
    pallas_call x1, Pallas kernels, on_device(): pl.pallas_call(partial(kernel, (n_ctx, n_sec, n_exp, chunk)), out_shape=[...  20.9 us
    pallas_call x1, Pallas kernels, on_device(): pl.pallas_call(hand_out, out_shape=[jax.ShapeDtypeStruct((length, dim), B...  1.09 us

profile of v3, /device:TPU:0, one launch (start us, length us, event | category | flops | bytes accessed | tf_op | source)
XLA Modules:
  0.0 22.7 jit_solution(7311134629980824060)
XLA Ops:
  0.6 20.9 %shard_map.110 = (bf16[1024,128]{1,0:T(8,128)(2,1)S(1)}, bf16[1024,128]{1,0:T(8,128)(2,1)S(1)}, bf16[1024,128]{1,0:T(8,128)(2,1)S(1)}, bf16[1024,128]{1,0:T(8,128)(2,1)S(1)}, bf16[1024,128]{1,0:T(8,128)(2,1)S(1)}) custom-call(bf16[1024,128]{1,0:T(8,128)(2,1)} %q_h.1, bf16[1024,128]{1,0:T(8,128)(2,1)} %k_h.1, bf16[1024,128]{1,0:T(8,128)(2,1)} %v_h.1, ...), custom_call_target="tpu_custom_call" | custom-call | tf_op jit(solution)/shard_map/pallas_call | solution.py:285
  21.6 1.1 %shard_map.111 = (bf16[1024,128]{1,0:T(8,128)(2,1)}, bf16[1024,128]{1,0:T(8,128)(2,1)}, bf16[1024,128]{1,0:T(8,128)(2,1)}, bf16[1024,128]{1,0:T(8,128)(2,1)}, bf16[1024,128]{1,0:T(8,128)(2,1)}) custom-call(bf16[1024,128]{1,0:T(8,128)(2,1)S(1)} %get-tuple-element.10.refs_0_, bf16[1024,128]{1,0:T(8,128)(2,1)S(1)} %get-tuple-element.11.refs_1_, ...), custom_call_target="tpu_custom_call" | custom-call | tf_op jit(solution)/shard_map/pallas_call | solution.py:324

commit v4 on v3

--- a/solution.py
+++ b/solution.py
@@ -39,17 +39,20 @@
 def kernel(
     sizes,
     q_h, k_h, v_h, gi_h, go_h, gain_h, ld_h,
-    lo_h, gq_h, gk_h, gv_h, gg_h,
-    q, k, v, gi, go, lo, gq, gk, gv, gg,
-    gain_ref, ld_ref, steps, fd, tail, table, wq, attn, signal, gate, upd, ent, g, gkl, gvl,
+    lo, gq, gk, gv, gg,
+    q, k, v, gi, go,
+    gain_ref, ld_ref, steps, fd, tail, table, wq, attn, signal, gate, upd, ent, g, gkl, gvl, turned_q, inv_cols,
     fsend, frecv, bsend, brecv, acc, rsend, rrecv, coef,
-    in_sem, out_sem, fs_sem, fr_sem, bs_sem, br_sem, rs_sem, rr_sem,
+    in_sem, fs_sem, fr_sem, bs_sem, br_sem, rs_sem, rr_sem,
 ):
     n_ctx, n_sec, n_exp, chunk = sizes
     n_norm = n_sec * n_exp
     length, dim = q.shape
     count = length // chunk
     me = lax.axis_index("ctx")
+    pair = 2 if n_ctx % 2 == 0 else 1
+    n_row = n_ctx // pair
+    row, core = lax.div(me, pair), lax.rem(me, pair)
     sec = lax.axis_index("section")
     ex = lax.axis_index("exp")
     mine = sec * n_exp + ex
@@ -69,19 +72,14 @@
         loads[i].start()
 
     barrier = pltpu.get_barrier_semaphore()
-    for r in range(1, n_ctx):
-        pl.semaphore_signal(
-            barrier, inc=1, device_id={"ctx": lax.rem(me + r, n_ctx)}, device_id_type=MESH
-        )
+    for r in range(1, n_row):
+        other = lax.rem(row + r, n_row) * pair + core
+        pl.semaphore_signal(barrier, inc=1, device_id={"ctx": other}, device_id_type=MESH)
+    if pair == 2:
+        twin = row * pair + 1 - core
+        pl.semaphore_signal(barrier, inc=1, device_id={"ctx": twin}, device_id_type=MESH)
     for r in range(1, n_norm):
         pl.semaphore_signal(barrier, inc=1, device_id=norm_peer(r), device_id_type=MESH)
-
-    stores = [
-        pltpu.make_async_copy(src, dst, out_sem.at[i])
-        for i, (src, dst) in enumerate(
-            ((lo, lo_h), (gg, gg_h), (gq, gq_h), (gk, gk_h), (gv, gv_h))
-        )
-    ]
 
     rows = [pl.ds(c * chunk, chunk) for c in range(count)]
 
@@ -112,19 +110,87 @@
     fsend[0:dim, :] = local
     fsend[dim : dim + EXTRA, :] = jnp.broadcast_to(total, (EXTRA, dim))
 
-    pl.semaphore_wait(barrier, n_ctx - 1 + n_norm - 1)
-
-    def forward_copy(r):
-        return pltpu.make_async_remote_copy(
-            src_ref=fsend, dst_ref=frecv.at[r], send_sem=fs_sem.at[r], recv_sem=fr_sem.at[r],
-            device_id={"ctx": lax.rem(me + r, n_ctx)}, device_id_type=MESH,
-        )
-
-    def backward_copy(r):
-        return pltpu.make_async_remote_copy(
-            src_ref=bsend, dst_ref=brecv.at[r], send_sem=bs_sem.at[r], recv_sem=br_sem.at[r],
-            device_id={"ctx": lax.rem(me + n_ctx - r, n_ctx)}, device_id_type=MESH,
-        )
+    pl.semaphore_wait(barrier, n_row - 1 + pair - 1 + n_norm - 1)
+
+    def exchange(reverse, send, recv, s_sem, r_sem):
+        y, c = (n_row - 1 - row, pair - 1 - core) if reverse else (row, core)
+
+        def to(y_to, c_to):
+            if reverse:
+                y_to, c_to = n_row - 1 - y_to, pair - 1 - c_to
+            return {"ctx": y_to * pair + c_to}
+
+        def copy(src, slot, target):
+            return pltpu.make_async_remote_copy(
+                src_ref=src, dst_ref=recv.at[slot], send_sem=s_sem.at[slot],
+                recv_sem=r_sem.at[slot], device_id=target, device_id_type=MESH,
+            )
+
+        def direct(d):
+            return copy(send, d * pair, to(lax.rem(y + d, n_row), c))
+
+        def relay(d):
+            return copy(recv.at[d * pair], d * pair + 1, to(y, 1 - c))
+
+        def neighbour():
+            return copy(send, 1, to(y, 1 - c))
+
+        def start():
+            for d in range(1, n_row):
+                @pl.when(y + d < n_row)
+                def _(d=d):
+                    direct(d).start()
+            if pair == 2:
+                @pl.when(c == 0)
+                def _():
+                    neighbour().start()
+
+        def pass_on():
+            for d in range(1, n_row):
+                @pl.when(y >= d)
+                def _(d=d):
+                    direct(d).wait_recv()
+                    if pair == 2:
+                        relay(d).start()
+
+        def join(slot):
+            acc[...] = jnp.exp(recv[slot, dim : dim + 1, :]) * acc[...] + recv[slot, 0:dim, :]
+
+        def collect():
+            acc[...] = jnp.zeros_like(acc)
+            for d in range(n_row - 1, 0, -1):
+                @pl.when(y >= d)
+                def _(d=d):
+                    if pair == 2:
+                        relay(d).wait_recv()
+                        join(d * pair + c)
+                        join(d * pair + 1 - c)
+                    else:
+                        join(d)
+            if pair == 2:
+                @pl.when(c == 1)
+                def _():
+                    neighbour().wait_recv()
+                    join(1)
+
+        def finish():
+            for d in range(1, n_row):
+                @pl.when(y + d < n_row)
+                def _(d=d):
+                    direct(d).wait_send()
+                if pair == 2:
+                    @pl.when(y >= d)
+                    def _(d=d):
+                        relay(d).wait_send()
+            if pair == 2:
+                @pl.when(c == 0)
+                def _():
+                    neighbour().wait_send()
+
+        return start, pass_on, collect, finish
+
+    forward = exchange(False, fsend, frecv, fs_sem, fr_sem)
+    backward = exchange(True, bsend, brecv, bs_sem, br_sem)
 
     def row_copy(r):
         return pltpu.make_async_remote_copy(
@@ -132,10 +198,7 @@
             device_id=norm_peer(r), device_id_type=MESH,
         )
 
-    for r in range(1, n_ctx):
-        @pl.when(me + r < n_ctx)
-        def _(r=r):
-            forward_copy(r).start()
+    forward[0]()
 
     loads[2].wait()
     t_index = lax.broadcasted_iota(jnp.int32, (chunk, chunk), 0)
@@ -148,6 +211,7 @@
         scores = (mm(q[rows[c], :], k[rows[c], :], NT) * weights).astype(BF)
         wq[c] = scores
         attn[rows[c], :] = mm(scores, v[rows[c], :], NN)
+    forward[1]()
     loads[3].wait()
     loads[4].wait()
     loads[5].wait()
@@ -157,12 +221,7 @@
         gate[rows[c], :] = prob
         signal[rows[c], :] = go[rows[c], :].astype(F32) * prob * gain
 
-    acc[...] = jnp.zeros_like(acc)
-    for r in range(n_ctx - 1, 0, -1):
-        @pl.when(me >= r)
-        def _(r=r):
-            forward_copy(r).wait_recv()
-            acc[...] = jnp.exp(frecv[r, dim : dim + 1, :]) * acc[...] + frecv[r, 0:dim, :]
+    forward[2]()
 
     state = acc[...]
     ones = jnp.ones((8, dim), BF)
@@ -181,6 +240,10 @@
     for r in range(1, n_norm):
         row_copy(r).start()
     coef[...] = jnp.zeros_like(coef)
+    for c in range(count):
+        high, low = split(jnp.transpose(q[rows[c], :].astype(F32) * fd[rows[c], :]))
+        turned_q[c, 0:dim, :] = high
+        turned_q[c, dim : 2 * dim, :] = low
     sums = rsend[...]
     for r in range(1, n_norm):
         row_copy(r).wait_recv()
@@ -197,25 +260,16 @@
         full = attn[rows[c], :]
         grad = (inv_b * (signal[rows[c], :] - full * along_b)).astype(BF)
         g[rows[c], :] = grad
-        high, low = split(q[rows[c], :].astype(F32) * fd[rows[c], :])
-        seen[c] = mm(high, grad, TN) + mm(low, grad, TN)
+        inv_cols[rows[c], :] = inv_b
+        both = mm(turned_q[c], grad, NN)
+        seen[c] = both[0:dim, :] + both[dim : 2 * dim, :]
         upd[c] = seen[c]
-        scaled = full * inv_b * gain
-        prob = gate[rows[c], :]
-        out = scaled * prob
-        lo[rows[c], :] = out.astype(BF)
-        gg[rows[c], :] = (go[rows[c], :].astype(F32) * out * (1.0 - prob)).astype(BF)
     local = None
     for c in range(count - 1, -1, -1):
         local = seen[c] if local is None else jnp.exp(ends[c]) * local + seen[c]
     bsend[0:dim, :] = local
     bsend[dim : dim + EXTRA, :] = jnp.broadcast_to(total, (EXTRA, dim))
-    for r in range(1, n_ctx):
-        @pl.when(me >= r)
-        def _(r=r):
-            backward_copy(r).start()
-    stores[0].start()
-    stores[1].start()
+    backward[0]()
 
     for c in range(count):
         grad = g[rows[c], :]
@@ -227,14 +281,14 @@
         ).astype(BF)
         gkl[rows[c], :] = mm(dv, q[rows[c], :], TN)
         gvl[rows[c], :] = mm(wq[c], grad, TN)
-    stores[2].start()
-
-    acc[...] = jnp.zeros_like(acc)
-    for r in range(n_ctx - 1, 0, -1):
-        @pl.when(me + r < n_ctx)
-        def _(r=r):
-            backward_copy(r).wait_recv()
-            acc[...] = jnp.exp(brecv[r, dim : dim + 1, :]) * acc[...] + brecv[r, 0:dim, :]
+    backward[1]()
+    for c in range(count):
+        prob = gate[rows[c], :]
+        out = attn[rows[c], :] * inv_cols[rows[c], :] * gain * prob
+        lo[rows[c], :] = out.astype(BF)
+        gg[rows[c], :] = (go[rows[c], :].astype(F32) * out * (1.0 - prob)).astype(BF)
+
+    backward[2]()
 
     state = acc[...]
     for c in range(count - 1, -1, -1):
@@ -246,21 +300,11 @@
         gv[rows[c], :] = (gvl[rows[c], :] + fall * (mm(kc, high, NN) + mm(kc, low, NN))).astype(BF)
         if c > 0:
             state = jnp.exp(ends[c]) * state + upd[c]
-    stores[3].start()
-    stores[4].start()
-
-    for r in range(1, n_ctx):
-        @pl.when(me + r < n_ctx)
-        def _(r=r):
-            forward_copy(r).wait_send()
-
-        @pl.when(me >= r)
-        def _(r=r):
-            backward_copy(r).wait_send()
+
+    forward[3]()
+    backward[3]()
     for r in range(1, n_norm):
         row_copy(r).wait_send()
-    for copy in stores:
-        copy.wait()
 
 
 def hand_out(*refs):
@@ -284,10 +328,10 @@
     sem = lambda n: pltpu.SemaphoreType.DMA((n,))
     results = pl.pallas_call(
         partial(kernel, (n_ctx, n_sec, n_exp, chunk)),
-        out_shape=[jax.ShapeDtypeStruct((length, dim), BF)] * 5,
+        out_shape=[pltpu.VMEM((length, dim), BF)] * 5,
         in_specs=[hbm_spec] * 7,
-        out_specs=[any_spec] * 5,
-        scratch_shapes=[block(BF)] * 10
+        out_specs=[pl.BlockSpec(memory_space=pltpu.VMEM)] * 5,
+        scratch_shapes=[block(BF)] * 5
         + [
             pltpu.VMEM((1, dim), F32),
             pltpu.VMEM((1, length), F32),
@@ -303,6 +347,8 @@
             pltpu.VMEM((count, dim, 2 * dim), BF),
             block(BF),
             block(F32),
+            block(F32),
+            pltpu.VMEM((count, 2 * dim, chunk), BF),
             block(F32),
             pltpu.VMEM((dim + EXTRA, dim), F32),
             pltpu.VMEM((n_ctx, dim + EXTRA, dim), F32),
@@ -312,7 +358,7 @@
             pltpu.VMEM((2, length), F32),
             pltpu.VMEM((n_norm, 2, length), F32),
             pltpu.VMEM((8, length), F32),
-            sem(7), sem(5), sem(n_ctx), sem(n_ctx), sem(n_ctx), sem(n_ctx), sem(n_norm), sem(n_norm),
+            sem(7), sem(n_ctx), sem(n_ctx), sem(n_ctx), sem(n_ctx), sem(n_norm), sem(n_norm),
         ],
         compiler_params=pltpu.CompilerParams(
             collective_id=0, has_side_effects=True, vmem_limit_bytes=48 * 1024 * 1024

time: 22.9 us -> 22.1 us (0.965)
  Pallas kernels: 22 us -> 21.1 us
    pallas_call x1, Pallas kernels: 20.9 us -> 20 us  [on_device(): pl.pallas_call(partial(kernel, (n_ctx, n_sec, n_exp, chunk)), out_shape=[...]
where the time goes in v4:
time: 22.1 us; the launch traced here: 21.7 us
  Pallas kernels  21.1 us (95%)
  between operations  0.64 us (3%)
    pallas_call x1, Pallas kernels, on_device(): pl.pallas_call(partial(kernel, (n_ctx, n_sec, n_exp, chunk)), out_shape=[...  20 us
    pallas_call x1, Pallas kernels, on_device(): pl.pallas_call(hand_out, out_shape=[jax.ShapeDtypeStruct((length, dim), B...  1.09 us

profile of v4, /device:TPU:0, one launch (start us, length us, event | category | flops | bytes accessed | tf_op | source)
XLA Modules:
  0.0 21.7 jit_solution(15558288395620301607)
XLA Ops:
  0.6 20.0 %shard_map.110 = (bf16[1024,128]{1,0:T(8,128)(2,1)S(1)}, bf16[1024,128]{1,0:T(8,128)(2,1)S(1)}, bf16[1024,128]{1,0:T(8,128)(2,1)S(1)}, bf16[1024,128]{1,0:T(8,128)(2,1)S(1)}, bf16[1024,128]{1,0:T(8,128)(2,1)S(1)}) custom-call(bf16[1024,128]{1,0:T(8,128)(2,1)} %q_h.1, bf16[1024,128]{1,0:T(8,128)(2,1)} %k_h.1, bf16[1024,128]{1,0:T(8,128)(2,1)} %v_h.1, ...), custom_call_target="tpu_custom_call" | custom-call | tf_op jit(solution)/shard_map/pallas_call | solution.py:329
  20.6 1.1 %shard_map.111 = (bf16[1024,128]{1,0:T(8,128)(2,1)}, bf16[1024,128]{1,0:T(8,128)(2,1)}, bf16[1024,128]{1,0:T(8,128)(2,1)}, bf16[1024,128]{1,0:T(8,128)(2,1)}, bf16[1024,128]{1,0:T(8,128)(2,1)}) custom-call(bf16[1024,128]{1,0:T(8,128)(2,1)S(1)} %get-tuple-element.10.refs_0_, bf16[1024,128]{1,0:T(8,128)(2,1)S(1)} %get-tuple-element.11.refs_1_, ...), custom_call_target="tpu_custom_call" | custom-call | tf_op jit(solution)/shard_map/pallas_call | solution.py:370

commit v5 on v4

--- a/solution.py
+++ b/solution.py
@@ -41,7 +41,7 @@
     q_h, k_h, v_h, gi_h, go_h, gain_h, ld_h,
     lo, gq, gk, gv, gg,
     q, k, v, gi, go,
-    gain_ref, ld_ref, steps, fd, tail, table, wq, attn, signal, gate, upd, ent, g, gkl, gvl, turned_q, inv_cols,
+    gain_ref, ld_ref, steps, fd, tail, table, wq, attn, signal, gate, upd, ent, g, gkl, gvl, turned_q, inv_cols, cols, fall,
     fsend, frecv, bsend, brecv, acc, rsend, rrecv, coef,
     in_sem, fs_sem, fr_sem, bs_sem, br_sem, rs_sem, rr_sem,
 ):
@@ -93,8 +93,16 @@
     ends = [run[c : c + 1, chunk - 1 : chunk] for c in range(count)]
     for c in range(count):
         column = jnp.broadcast_to(run_t[:, c : c + 1], (chunk, dim))
-        fd[rows[c], :] = jnp.exp(column)
+        cols[rows[c], :] = column
         tail[rows[c], :] = jnp.exp(ends[c] - column)
+        fall[c : c + 1, :] = jnp.broadcast_to(jnp.exp(ends[c]), (1, dim))
+
+    def each(body):
+        def one(c, carry):
+            body(c, pl.ds(pl.multiple_of(c * chunk, chunk), chunk))
+            return carry
+
+        lax.fori_loop(0, count, one, 0)
 
     loads[0].wait()
     loads[1].wait()
@@ -203,47 +211,59 @@
     loads[2].wait()
     t_index = lax.broadcasted_iota(jnp.int32, (chunk, chunk), 0)
     s_index = lax.broadcasted_iota(jnp.int32, (chunk, chunk), 1)
-    for c in range(count):
-        column = jnp.broadcast_to(run_t[:, c : c + 1], (chunk, chunk))
-        gap = jnp.minimum(column - steps[c : c + 1, :], 0.0)
+
+    def inside(c, here):
+        column = cols[here, :]
+        fd[here, :] = jnp.exp(column)
+        column = jnp.concatenate([column] * (chunk // dim), axis=1) if chunk >= dim else column[:, :chunk]
+        gap = jnp.minimum(column - steps[pl.ds(c, 1), :], 0.0)
         weights = jnp.where(t_index >= s_index, jnp.exp(gap), 0.0)
         table[c] = weights
-        scores = (mm(q[rows[c], :], k[rows[c], :], NT) * weights).astype(BF)
+        scores = (mm(q[here, :], k[here, :], NT) * weights).astype(BF)
         wq[c] = scores
-        attn[rows[c], :] = mm(scores, v[rows[c], :], NN)
+        attn[here, :] = mm(scores, v[here, :], NN)
+
+    each(inside)
     forward[1]()
     loads[3].wait()
     loads[4].wait()
     loads[5].wait()
     gain = gain_ref[...]
-    for c in range(count):
-        prob = jax.nn.sigmoid(gi[rows[c], :].astype(F32))
-        gate[rows[c], :] = prob
-        signal[rows[c], :] = go[rows[c], :].astype(F32) * prob * gain
+
+    def gating(c, here):
+        prob = jax.nn.sigmoid(gi[here, :].astype(F32))
+        gate[here, :] = prob
+        signal[here, :] = go[here, :].astype(F32) * prob * gain
+
+    each(gating)
 
     forward[2]()
 
-    state = acc[...]
     ones = jnp.ones((8, dim), BF)
-    for c in range(count):
+
+    def attending(c, here):
+        state = acc[...]
         high, low = split(state)
+        both = mm(q[here, :], jnp.concatenate([high, low], axis=1), NN)
         ent[c, :, 0:dim] = high
         ent[c, :, dim : 2 * dim] = low
-        both = mm(q[rows[c], :], ent[c], NN)
-        full = attn[rows[c], :] + fd[rows[c], :] * (both[:, 0:dim] + both[:, dim : 2 * dim])
-        attn[rows[c], :] = full
-        rsend[0:1, rows[c]] = mm(ones, (full * full).astype(BF), NT)[0:1, :]
-        rsend[1:2, rows[c]] = mm(ones, (signal[rows[c], :] * full).astype(BF), NT)[0:1, :]
-        if c + 1 < count:
-            state = jnp.exp(ends[c]) * state + upd[c]
-
+        full = attn[here, :] + fd[here, :] * (both[:, 0:dim] + both[:, dim : 2 * dim])
+        attn[here, :] = full
+        rsend[0:1, here] = mm(ones, (full * full).astype(BF), NT)[0:1, :]
+        rsend[1:2, here] = mm(ones, (signal[here, :] * full).astype(BF), NT)[0:1, :]
+        acc[...] = fall[pl.ds(c, 1), :] * state + upd[c]
+
+    each(attending)
     for r in range(1, n_norm):
         row_copy(r).start()
     coef[...] = jnp.zeros_like(coef)
-    for c in range(count):
-        high, low = split(jnp.transpose(q[rows[c], :].astype(F32) * fd[rows[c], :]))
+
+    def turning(c, here):
+        high, low = split(jnp.transpose(q[here, :].astype(F32) * fd[here, :]))
         turned_q[c, 0:dim, :] = high
         turned_q[c, dim : 2 * dim, :] = low
+
+    each(turning)
     sums = rsend[...]
     for r in range(1, n_norm):
         row_copy(r).wait_recv()
@@ -252,54 +272,63 @@
     coef[0:1, :] = inv
     coef[1:2, :] = inv * inv * (sums[1:2, :] / width)
 
-    seen = [None] * count
-    for c in range(count):
-        turned = jnp.transpose(coef[:, rows[c]])
+    bsend[0:dim, :] = jnp.zeros((dim, dim), F32)
+
+    def grading(turn, carry):
+        c = count - 1 - turn
+        here = pl.ds(pl.multiple_of(c * chunk, chunk), chunk)
+        turned = jnp.transpose(coef[:, here])
         inv_b = jnp.broadcast_to(turned[:, 0:1], (chunk, dim))
         along_b = jnp.broadcast_to(turned[:, 1:2], (chunk, dim))
-        full = attn[rows[c], :]
-        grad = (inv_b * (signal[rows[c], :] - full * along_b)).astype(BF)
-        g[rows[c], :] = grad
-        inv_cols[rows[c], :] = inv_b
+        grad = (inv_b * (signal[here, :] - attn[here, :] * along_b)).astype(BF)
+        g[here, :] = grad
+        inv_cols[here, :] = inv_b
         both = mm(turned_q[c], grad, NN)
-        seen[c] = both[0:dim, :] + both[dim : 2 * dim, :]
-        upd[c] = seen[c]
-    local = None
-    for c in range(count - 1, -1, -1):
-        local = seen[c] if local is None else jnp.exp(ends[c]) * local + seen[c]
-    bsend[0:dim, :] = local
+        seen = both[0:dim, :] + both[dim : 2 * dim, :]
+        upd[c] = seen
+        bsend[0:dim, :] = fall[pl.ds(c, 1), :] * bsend[0:dim, :] + seen
+        return carry
+
+    lax.fori_loop(0, count, grading, 0)
     bsend[dim : dim + EXTRA, :] = jnp.broadcast_to(total, (EXTRA, dim))
     backward[0]()
 
-    for c in range(count):
-        grad = g[rows[c], :]
-        dv = (mm(grad, v[rows[c], :], NT) * table[c]).astype(BF)
+    def products(c, here):
+        grad = g[here, :]
+        dv = (mm(grad, v[here, :], NT) * table[c]).astype(BF)
         high = mm(grad, ent[c, :, 0:dim], NT)
         low = mm(grad, ent[c, :, dim : 2 * dim], NT)
-        gq[rows[c], :] = (
-            mm(dv, k[rows[c], :], NN) + fd[rows[c], :] * (high + low)
-        ).astype(BF)
-        gkl[rows[c], :] = mm(dv, q[rows[c], :], TN)
-        gvl[rows[c], :] = mm(wq[c], grad, TN)
+        gq[here, :] = (mm(dv, k[here, :], NN) + fd[here, :] * (high + low)).astype(BF)
+        gkl[here, :] = mm(dv, q[here, :], TN)
+        gvl[here, :] = mm(wq[c], grad, TN)
+
+    each(products)
     backward[1]()
-    for c in range(count):
-        prob = gate[rows[c], :]
-        out = attn[rows[c], :] * inv_cols[rows[c], :] * gain * prob
-        lo[rows[c], :] = out.astype(BF)
-        gg[rows[c], :] = (go[rows[c], :].astype(F32) * out * (1.0 - prob)).astype(BF)
+
+    def gated(c, here):
+        prob = gate[here, :]
+        out = attn[here, :] * inv_cols[here, :] * gain * prob
+        lo[here, :] = out.astype(BF)
+        gg[here, :] = (go[here, :].astype(F32) * out * (1.0 - prob)).astype(BF)
+
+    each(gated)
 
     backward[2]()
 
-    state = acc[...]
-    for c in range(count - 1, -1, -1):
+    def finishing(turn, carry):
+        c = count - 1 - turn
+        here = pl.ds(pl.multiple_of(c * chunk, chunk), chunk)
+        state = acc[...]
         high, low = split(state)
-        fall = tail[rows[c], :]
-        vc = v[rows[c], :]
-        kc = k[rows[c], :]
-        gk[rows[c], :] = (gkl[rows[c], :] + fall * (mm(vc, high, NT) + mm(vc, low, NT))).astype(BF)
-        gv[rows[c], :] = (gvl[rows[c], :] + fall * (mm(kc, high, NN) + mm(kc, low, NN))).astype(BF)
-        if c > 0:
-            state = jnp.exp(ends[c]) * state + upd[c]
+        left = tail[here, :]
+        vc = v[here, :]
+        kc = k[here, :]
+        gk[here, :] = (gkl[here, :] + left * (mm(vc, high, NT) + mm(vc, low, NT))).astype(BF)
+        gv[here, :] = (gvl[here, :] + left * (mm(kc, high, NN) + mm(kc, low, NN))).astype(BF)
+        acc[...] = fall[pl.ds(c, 1), :] * state + upd[c]
+        return carry
+
+    lax.fori_loop(0, count, finishing, 0)
 
     forward[3]()
     backward[3]()
@@ -350,6 +379,8 @@
             block(F32),
             pltpu.VMEM((count, 2 * dim, chunk), BF),
             block(F32),
+            block(F32),
+            pltpu.VMEM((8, dim), F32),
             pltpu.VMEM((dim + EXTRA, dim), F32),
             pltpu.VMEM((n_ctx, dim + EXTRA, dim), F32),
             pltpu.VMEM((dim + EXTRA, dim), F32),

time: 22.1 us -> 24 us (1.086)
  Pallas kernels: 21.1 us -> 22.9 us
    pallas_call x1, Pallas kernels: 20 us -> 21.9 us  [on_device(): pl.pallas_call(partial(kernel, (n_ctx, n_sec, n_exp, chunk)), out_shape=[...]
where the time goes in v5:
time: 24 us; the launch traced here: 23.6 us
  Pallas kernels  22.9 us (95%)
  between operations  0.64 us (3%)
    pallas_call x1, Pallas kernels, on_device(): pl.pallas_call(partial(kernel, (n_ctx, n_sec, n_exp, chunk)), out_shape=[...  21.9 us
    pallas_call x1, Pallas kernels, on_device(): pl.pallas_call(hand_out, out_shape=[jax.ShapeDtypeStruct((length, dim), B...  1.09 us

profile of v5, /device:TPU:0, one launch (start us, length us, event | category | flops | bytes accessed | tf_op | source)
XLA Modules:
  0.0 23.6 jit_solution(838636008529584011)
XLA Ops:
  0.6 21.9 %shard_map.110 = (bf16[1024,128]{1,0:T(8,128)(2,1)S(1)}, bf16[1024,128]{1,0:T(8,128)(2,1)S(1)}, bf16[1024,128]{1,0:T(8,128)(2,1)S(1)}, bf16[1024,128]{1,0:T(8,128)(2,1)S(1)}, bf16[1024,128]{1,0:T(8,128)(2,1)S(1)}) custom-call(bf16[1024,128]{1,0:T(8,128)(2,1)} %q_h.1, bf16[1024,128]{1,0:T(8,128)(2,1)} %k_h.1, bf16[1024,128]{1,0:T(8,128)(2,1)} %v_h.1, ...), custom_call_target="tpu_custom_call" | custom-call | tf_op jit(solution)/shard_map/pallas_call | solution.py:358
  22.5 1.1 %shard_map.111 = (bf16[1024,128]{1,0:T(8,128)(2,1)}, bf16[1024,128]{1,0:T(8,128)(2,1)}, bf16[1024,128]{1,0:T(8,128)(2,1)}, bf16[1024,128]{1,0:T(8,128)(2,1)}, bf16[1024,128]{1,0:T(8,128)(2,1)}) custom-call(bf16[1024,128]{1,0:T(8,128)(2,1)S(1)} %get-tuple-element.10.refs_0_, bf16[1024,128]{1,0:T(8,128)(2,1)S(1)} %get-tuple-element.11.refs_1_, ...), custom_call_target="tpu_custom_call" | custom-call | tf_op jit(solution)/shard_map/pallas_call | solution.py:401

commit v6 on v4

--- a/solution.py
+++ b/solution.py
@@ -28,12 +28,13 @@
 
 
 def prefix_rows(x):
-    lane = lax.broadcasted_iota(jnp.int32, x.shape, 1)
-    shift = 1
-    while shift < x.shape[1]:
-        x = x + jnp.where(lane >= shift, pltpu.roll(x, shift, 1), 0.0)
-        shift *= 2
-    return x
+    size = x.shape[1]
+    first = lax.broadcasted_iota(jnp.int32, (size, size), 0)
+    last = lax.broadcasted_iota(jnp.int32, (size, size), 1)
+    upto = jnp.where(first <= last, 1.0, 0.0).astype(BF)
+    high, low = split(x)
+    rest = (x - high.astype(F32) - low.astype(F32)).astype(BF)
+    return mm(high, upto, NN) + (mm(low, upto, NN) + mm(rest, upto, NN))
 
 
 def kernel(
@@ -93,7 +94,6 @@
     ends = [run[c : c + 1, chunk - 1 : chunk] for c in range(count)]
     for c in range(count):
         column = jnp.broadcast_to(run_t[:, c : c + 1], (chunk, dim))
-        fd[rows[c], :] = jnp.exp(column)
         tail[rows[c], :] = jnp.exp(ends[c] - column)
 
     loads[0].wait()
@@ -192,9 +192,10 @@
     forward = exchange(False, fsend, frecv, fs_sem, fr_sem)
     backward = exchange(True, bsend, brecv, bs_sem, br_sem)
 
-    def row_copy(r):
+    def row_copy(half, r):
+        slot = half * n_norm + r
         return pltpu.make_async_remote_copy(
-            src_ref=rsend, dst_ref=rrecv.at[r], send_sem=rs_sem.at[r], recv_sem=rr_sem.at[r],
+            src_ref=rsend.at[half], dst_ref=rrecv.at[slot], send_sem=rs_sem.at[slot], recv_sem=rr_sem.at[slot],
             device_id=norm_peer(r), device_id_type=MESH,
         )
 
@@ -205,6 +206,7 @@
     s_index = lax.broadcasted_iota(jnp.int32, (chunk, chunk), 1)
     for c in range(count):
         column = jnp.broadcast_to(run_t[:, c : c + 1], (chunk, chunk))
+        fd[rows[c], :] = jnp.exp(column[:, 0:dim])
         gap = jnp.minimum(column - steps[c : c + 1, :], 0.0)
         weights = jnp.where(t_index >= s_index, jnp.exp(gap), 0.0)
         table[c] = weights
@@ -221,39 +223,46 @@
         gate[rows[c], :] = prob
         signal[rows[c], :] = go[rows[c], :].astype(F32) * prob * gain
 
+    for c in range(count):
+        high, low = split(jnp.transpose(q[rows[c], :].astype(F32) * fd[rows[c], :]))
+        turned_q[c, 0:dim, :] = high
+        turned_q[c, dim : 2 * dim, :] = low
+
     forward[2]()
 
     state = acc[...]
     ones = jnp.ones((8, dim), BF)
-    for c in range(count):
+    halves = rsend.shape[0]
+    per = count // halves
+    for c in range(count):
+        half, part = c // per, pl.ds((c % per) * chunk, chunk)
         high, low = split(state)
         ent[c, :, 0:dim] = high
         ent[c, :, dim : 2 * dim] = low
         both = mm(q[rows[c], :], ent[c], NN)
         full = attn[rows[c], :] + fd[rows[c], :] * (both[:, 0:dim] + both[:, dim : 2 * dim])
         attn[rows[c], :] = full
-        rsend[0:1, rows[c]] = mm(ones, (full * full).astype(BF), NT)[0:1, :]
-        rsend[1:2, rows[c]] = mm(ones, (signal[rows[c], :] * full).astype(BF), NT)[0:1, :]
+        rsend[half, 0:1, part] = mm(ones, (full * full).astype(BF), NT)[0:1, :]
+        rsend[half, 1:2, part] = mm(ones, (signal[rows[c], :] * full).astype(BF), NT)[0:1, :]
         if c + 1 < count:
             state = jnp.exp(ends[c]) * state + upd[c]
-
-    for r in range(1, n_norm):
-        row_copy(r).start()
+        if c % per == per - 1:
+            for r in range(1, n_norm):
+                row_copy(half, r).start()
+
     coef[...] = jnp.zeros_like(coef)
-    for c in range(count):
-        high, low = split(jnp.transpose(q[rows[c], :].astype(F32) * fd[rows[c], :]))
-        turned_q[c, 0:dim, :] = high
-        turned_q[c, dim : 2 * dim, :] = low
-    sums = rsend[...]
-    for r in range(1, n_norm):
-        row_copy(r).wait_recv()
-        sums = sums + rrecv[r]
-    inv = lax.rsqrt(sums[0:1, :] / width + epsilon)
-    coef[0:1, :] = inv
-    coef[1:2, :] = inv * inv * (sums[1:2, :] / width)
-
     seen = [None] * count
     for c in range(count):
+        half = c // per
+        if c % per == 0:
+            sums = rsend[half]
+            for r in range(1, n_norm):
+                row_copy(half, r).wait_recv()
+                sums = sums + rrecv[half * n_norm + r]
+            inv = lax.rsqrt(sums[0:1, :] / width + epsilon)
+            here = pl.ds(half * per * chunk, per * chunk)
+            coef[0:1, here] = inv
+            coef[1:2, here] = inv * inv * (sums[1:2, :] / width)
         turned = jnp.transpose(coef[:, rows[c]])
         inv_b = jnp.broadcast_to(turned[:, 0:1], (chunk, dim))
         along_b = jnp.broadcast_to(turned[:, 1:2], (chunk, dim))
@@ -293,18 +302,23 @@
     state = acc[...]
     for c in range(count - 1, -1, -1):
         high, low = split(state)
+        wide = jnp.concatenate([high, low], axis=1)
+        tall = jnp.concatenate([high, low], axis=0)
         fall = tail[rows[c], :]
         vc = v[rows[c], :]
         kc = k[rows[c], :]
-        gk[rows[c], :] = (gkl[rows[c], :] + fall * (mm(vc, high, NT) + mm(vc, low, NT))).astype(BF)
-        gv[rows[c], :] = (gvl[rows[c], :] + fall * (mm(kc, high, NN) + mm(kc, low, NN))).astype(BF)
+        from_v = mm(vc, tall, NT)
+        from_k = mm(kc, wide, NN)
+        gk[rows[c], :] = (gkl[rows[c], :] + fall * (from_v[:, 0:dim] + from_v[:, dim : 2 * dim])).astype(BF)
+        gv[rows[c], :] = (gvl[rows[c], :] + fall * (from_k[:, 0:dim] + from_k[:, dim : 2 * dim])).astype(BF)
         if c > 0:
             state = jnp.exp(ends[c]) * state + upd[c]
 
     forward[3]()
     backward[3]()
-    for r in range(1, n_norm):
-        row_copy(r).wait_send()
+    for half in range(halves):
+        for r in range(1, n_norm):
+            row_copy(half, r).wait_send()
 
 
 def hand_out(*refs):
@@ -322,6 +336,7 @@
     count = length // chunk
     assert count * chunk == length and count <= 8
     n_norm = n_sec * n_exp
+    halves = 2 if count % 2 == 0 else 1
     any_spec = pl.BlockSpec(memory_space=pl.ANY)
     hbm_spec = pl.BlockSpec(memory_space=pltpu.HBM)
     block = lambda dtype: pltpu.VMEM((length, dim), dtype)
@@ -355,10 +370,10 @@
             pltpu.VMEM((dim + EXTRA, dim), F32),
             pltpu.VMEM((n_ctx, dim + EXTRA, dim), F32),
             pltpu.VMEM((dim, dim), F32),
-            pltpu.VMEM((2, length), F32),
-            pltpu.VMEM((n_norm, 2, length), F32),
+            pltpu.VMEM((halves, 2, length // halves), F32),
+            pltpu.VMEM((halves * n_norm, 2, length // halves), F32),
             pltpu.VMEM((8, length), F32),
-            sem(7), sem(n_ctx), sem(n_ctx), sem(n_ctx), sem(n_ctx), sem(n_norm), sem(n_norm),
+            sem(7), sem(n_ctx), sem(n_ctx), sem(n_ctx), sem(n_ctx), sem(halves * n_norm), sem(halves * n_norm),
         ],
         compiler_params=pltpu.CompilerParams(
             collective_id=0, has_side_effects=True, vmem_limit_bytes=48 * 1024 * 1024

time: 22.1 us -> 21.8 us (0.986)
  the two profiles are of different devices: /device:TPU:0 before, /device:TPU:1 now
where the time goes in v6:
time: 21.8 us; the launch traced here: 21.6 us
  Pallas kernels  21 us (96%)
  between operations  0.64 us (3%)
    pallas_call x1, Pallas kernels, on_device(): pl.pallas_call(partial(kernel, (n_ctx, n_sec, n_exp, chunk)), out_shape=[...  19.9 us
    pallas_call x1, Pallas kernels, on_device(): pl.pallas_call(hand_out, out_shape=[jax.ShapeDtypeStruct((length, dim), B...  1.09 us

profile of v6, /device:TPU:1, one launch (start us, length us, event | category | flops | bytes accessed | tf_op | source)
XLA Modules:
  0.0 21.6 jit_solution(904322602606784417)
XLA Ops:
  0.6 19.9 %shard_map.110 = (bf16[1024,128]{1,0:T(8,128)(2,1)S(1)}, bf16[1024,128]{1,0:T(8,128)(2,1)S(1)}, bf16[1024,128]{1,0:T(8,128)(2,1)S(1)}, bf16[1024,128]{1,0:T(8,128)(2,1)S(1)}, bf16[1024,128]{1,0:T(8,128)(2,1)S(1)}) custom-call(bf16[1024,128]{1,0:T(8,128)(2,1)} %q_h.1, bf16[1024,128]{1,0:T(8,128)(2,1)} %k_h.1, bf16[1024,128]{1,0:T(8,128)(2,1)} %v_h.1, ...), custom_call_target="tpu_custom_call" | custom-call | tf_op jit(solution)/shard_map/pallas_call | solution.py:344
  20.5 1.1 %shard_map.111 = (bf16[1024,128]{1,0:T(8,128)(2,1)}, bf16[1024,128]{1,0:T(8,128)(2,1)}, bf16[1024,128]{1,0:T(8,128)(2,1)}, bf16[1024,128]{1,0:T(8,128)(2,1)}, bf16[1024,128]{1,0:T(8,128)(2,1)}) custom-call(bf16[1024,128]{1,0:T(8,128)(2,1)S(1)} %get-tuple-element.10.refs_0_, bf16[1024,128]{1,0:T(8,128)(2,1)S(1)} %get-tuple-element.11.refs_1_, ...), custom_call_target="tpu_custom_call" | custom-call | tf_op jit(solution)/shard_map/pallas_call | solution.py:385

commit v7 on v6

--- a/solution.py
+++ b/solution.py
@@ -20,6 +20,10 @@
 
 def mm(a, b, dims):
     return lax.dot_general(a, b, dims, preferred_element_type=F32)
+
+
+def pieces(dim):
+    return ((0, dim // 2), (dim // 2, dim - dim // 2 + EXTRA))
 
 
 def split(x):
@@ -120,38 +124,43 @@
                 y_to, c_to = n_row - 1 - y_to, pair - 1 - c_to
             return {"ctx": y_to * pair + c_to}
 
-        def copy(src, slot, target):
+        def copy(src, slot, target, part):
+            rows_of = pl.ds(*pieces(dim)[part])
             return pltpu.make_async_remote_copy(
-                src_ref=src, dst_ref=recv.at[slot], send_sem=s_sem.at[slot],
-                recv_sem=r_sem.at[slot], device_id=target, device_id_type=MESH,
+                src_ref=src.at[rows_of], dst_ref=recv.at[slot, rows_of],
+                send_sem=s_sem.at[2 * slot + part], recv_sem=r_sem.at[2 * slot + part],
+                device_id=target, device_id_type=MESH,
             )
 
-        def direct(d):
-            return copy(send, d * pair, to(lax.rem(y + d, n_row), c))
-
-        def relay(d):
-            return copy(recv.at[d * pair], d * pair + 1, to(y, 1 - c))
-
-        def neighbour():
-            return copy(send, 1, to(y, 1 - c))
+        def direct(d, part):
+            return copy(send, d * pair, to(lax.rem(y + d, n_row), c), part)
+
+        def relay(d, part):
+            return copy(recv.at[d * pair], d * pair + 1, to(y, 1 - c), part)
+
+        def neighbour(part):
+            return copy(send, 1, to(y, 1 - c), part)
 
         def start():
             for d in range(1, n_row):
                 @pl.when(y + d < n_row)
                 def _(d=d):
-                    direct(d).start()
+                    for part in range(2):
+                        direct(d, part).start()
             if pair == 2:
                 @pl.when(c == 0)
                 def _():
-                    neighbour().start()
+                    for part in range(2):
+                        neighbour(part).start()
 
         def pass_on():
             for d in range(1, n_row):
                 @pl.when(y >= d)
                 def _(d=d):
-                    direct(d).wait_recv()
-                    if pair == 2:
-                        relay(d).start()
+                    for part in range(2):
+                        direct(d, part).wait_recv()
+                        if pair == 2:
+                            relay(d, part).start()
 
         def join(slot):
             acc[...] = jnp.exp(recv[slot, dim : dim + 1, :]) * acc[...] + recv[slot, 0:dim, :]
@@ -162,7 +171,8 @@
                 @pl.when(y >= d)
                 def _(d=d):
                     if pair == 2:
-                        relay(d).wait_recv()
+                        for part in range(2):
+                            relay(d, part).wait_recv()
                         join(d * pair + c)
                         join(d * pair + 1 - c)
                     else:
@@ -170,22 +180,26 @@
             if pair == 2:
                 @pl.when(c == 1)
                 def _():
-                    neighbour().wait_recv()
+                    for part in range(2):
+                        neighbour(part).wait_recv()
                     join(1)
 
         def finish():
             for d in range(1, n_row):
                 @pl.when(y + d < n_row)
                 def _(d=d):
-                    direct(d).wait_send()
+                    for part in range(2):
+                        direct(d, part).wait_send()
                 if pair == 2:
                     @pl.when(y >= d)
                     def _(d=d):
-                        relay(d).wait_send()
+                        for part in range(2):
+                            relay(d, part).wait_send()
             if pair == 2:
                 @pl.when(c == 0)
                 def _():
-                    neighbour().wait_send()
+                    for part in range(2):
+                        neighbour(part).wait_send()
 
         return start, pass_on, collect, finish
 
@@ -373,7 +387,7 @@
             pltpu.VMEM((halves, 2, length // halves), F32),
             pltpu.VMEM((halves * n_norm, 2, length // halves), F32),
             pltpu.VMEM((8, length), F32),
-            sem(7), sem(n_ctx), sem(n_ctx), sem(n_ctx), sem(n_ctx), sem(halves * n_norm), sem(halves * n_norm),
+            sem(7), sem(2 * n_ctx), sem(2 * n_ctx), sem(2 * n_ctx), sem(2 * n_ctx), sem(halves * n_norm), sem(halves * n_norm),
         ],
         compiler_params=pltpu.CompilerParams(
             collective_id=0, has_side_effects=True, vmem_limit_bytes=48 * 1024 * 1024

time: 21.8 us -> 21.9 us (level)
  no operation moved by 1% of the time
where the time goes in v7:
time: 21.9 us; the launch traced here: 21.7 us
  Pallas kernels  21.1 us (96%)
  between operations  0.64 us (3%)
    pallas_call x1, Pallas kernels, on_device(): pl.pallas_call(partial(kernel, (n_ctx, n_sec, n_exp, chunk)), out_shape=[...  20 us
    pallas_call x1, Pallas kernels, on_device(): pl.pallas_call(hand_out, out_shape=[jax.ShapeDtypeStruct((length, dim), B...  1.09 us

profile of v7, /device:TPU:1, one launch (start us, length us, event | category | flops | bytes accessed | tf_op | source)
XLA Modules:
  0.0 21.7 jit_solution(4580095454579127251)
XLA Ops:
  0.6 20.0 %shard_map.110 = (bf16[1024,128]{1,0:T(8,128)(2,1)S(1)}, bf16[1024,128]{1,0:T(8,128)(2,1)S(1)}, bf16[1024,128]{1,0:T(8,128)(2,1)S(1)}, bf16[1024,128]{1,0:T(8,128)(2,1)S(1)}, bf16[1024,128]{1,0:T(8,128)(2,1)S(1)}) custom-call(bf16[1024,128]{1,0:T(8,128)(2,1)} %q_h.1, bf16[1024,128]{1,0:T(8,128)(2,1)} %k_h.1, bf16[1024,128]{1,0:T(8,128)(2,1)} %v_h.1, ...), custom_call_target="tpu_custom_call" | custom-call | tf_op jit(solution)/shard_map/pallas_call | solution.py:358
  20.6 1.1 %shard_map.111 = (bf16[1024,128]{1,0:T(8,128)(2,1)}, bf16[1024,128]{1,0:T(8,128)(2,1)}, bf16[1024,128]{1,0:T(8,128)(2,1)}, bf16[1024,128]{1,0:T(8,128)(2,1)}, bf16[1024,128]{1,0:T(8,128)(2,1)}) custom-call(bf16[1024,128]{1,0:T(8,128)(2,1)S(1)} %get-tuple-element.10.refs_0_, bf16[1024,128]{1,0:T(8,128)(2,1)S(1)} %get-tuple-element.11.refs_1_, ...), custom_call_target="tpu_custom_call" | custom-call | tf_op jit(solution)/shard_map/pallas_call | solution.py:399
